TPU v7x, 256 devices: a whole 4x4x8 slice. The times are simulated.
256 devices in a mesh: section: 2 (over x_hi), cp: 32 (over x_lo, z, core), fold: 4 (over y).
Axes of the slice: x: 4 (x_hi: 2, x_lo: 2; x = x_hi * 2 + x_lo), y: 4, z: 8, core: 2. Of those that a mesh axis runs over, the one named last changes fastest.
Arguments:
- activations: bfloat16 [2, 4096, 4096], P('section', 'cp', 'fold'), may hold values from -4 to 4
- queries: bfloat16 [2, 4096, 4096], P('section', 'cp', 'fold'), may hold values from -150 to 150
- keys: bfloat16 [2, 4096, 512], P('section', 'cp', 'fold'), may hold values from -6 to 6
- values: bfloat16 [2, 4096, 512], P('section', 'cp', 'fold'), may hold values from -6 to 6
- segments: int32 [2, 4096], P('section', 'cp'), may hold values from 0 to 7, never falling along the last dimension, each value on 1 to 2048 neighbouring positions
- routes: int32 [2, 4096, 8], P('section', 'cp'), may hold values from 0 to 63, all different within a row; in each aligned block of 128 rows (0 to 127, 128 to 255, ..., all dimensions but the last counted through in order) at most 20 rows name the same one
- route_weight: float32 [2, 4096, 8], P('section', 'cp'), may hold values from 0.1 to 1
- norm_gain: bfloat16 [2, 4096], P('section', 'fold'), may hold values from 0.25 to 4
- w_out: bfloat16 [2, 4096, 4096], P('section', 'fold', 'cp'), may hold values from -0.1875 to 0.1875
- w_gate: bfloat16 [2, 64, 768, 4096], P('section', 'cp', 'fold'), may hold values from -0.09375 to 0.09375
- w_up: bfloat16 [2, 64, 768, 4096], P('section', 'cp', 'fold'), may hold values from -0.09375 to 0.09375
- w_down: bfloat16 [2, 64, 768, 4096], P('section', 'cp', None, 'fold'), may hold values from -0.21875 to 0.21875
Outputs:
- passed: bfloat16 [2, 4096, 4096], P('section', 'cp', 'fold')
- passed_segments: int32 [2, 4096], P('section', 'cp')
Inputs may be any that keep to these rules, and one draw needn't show every extreme that they name: `routes`: within the tokens of one index of cp of one section (aligned blocks of 128 rows), no expert is named more than 20 times, a bound that some block reaches. `segments`: document ids never fall along a section's tokens; a document has at most 2048 tokens.
All inputs are finite; a program needn't handle non-finite values.
Results may differ from a plain program's by a relative error of at most 0.02.
Values may be sent and summed in bfloat16 or wider, within the bound.
A program may use at most 128 MiB of HBM per device.

v0:
```python
import math

import jax
import jax.numpy as jnp
from jax import lax
from jax.sharding import PartitionSpec as P

HEAD_SIZE = 128


NEG = -1e30
EPS = 1e-06


def shifted(array, axis, by):
    devices = lax.axis_size(axis)
    return lax.ppermute(array, axis, [(i, (i + by) % devices) for i in range(devices)])


def capacity_of(tok_rows, top_count, experts):
    return min(tok_rows, max(2, 5 * tok_rows * top_count // (4 * experts)))


def slot_places(routes, experts, capacity):
    flat = routes.reshape(-1)
    hits = (flat[:, None] == jnp.arange(experts, dtype=jnp.int32)[None, :]).astype(jnp.int32)
    rank = jnp.sum((jnp.cumsum(hits, axis=0) - 1) * hits, axis=1)
    return flat * capacity + rank


def attend(query, keys, values, segment):
    tok_rows = query.shape[0]
    kv_dev = keys.shape[1] // HEAD_SIZE
    query_group = query.shape[1] // keys.shape[1]
    q_heads = query.reshape(tok_rows, kv_dev, query_group, HEAD_SIZE)
    q_place = lax.axis_index("cp") * tok_rows + jnp.arange(tok_rows, dtype=jnp.int32)
    scale = 1.0 / math.sqrt(HEAD_SIZE)
    start_top = jnp.full((tok_rows, kv_dev, query_group), NEG, jnp.float32)
    top = start_top
    k_piece = lax.all_gather(keys, "cp", axis=0, tiled=True)
    v_piece = lax.all_gather(values, "cp", axis=0, tiled=True)
    s_piece = lax.all_gather(segment, "cp", axis=0, tiled=True)
    count = k_piece.shape[0]
    key_heads = k_piece.reshape(count, kv_dev, HEAD_SIZE)
    value_heads = v_piece.reshape(count, kv_dev, HEAD_SIZE)
    score = (
        jnp.einsum("tkgd,nkd->tkgn", q_heads, key_heads, preferred_element_type=jnp.float32) * scale
    )
    k_place = jnp.arange(count, dtype=jnp.int32)
    allowed = (k_place[None, :] <= q_place[:, None]) & (s_piece[None, :] == segment[:, None])
    allowed = allowed[:, None, None, :]
    score = jnp.where(allowed, score, NEG)
    new_top = jnp.maximum(top, jnp.max(score, axis=-1))
    weight = jnp.where(allowed, jnp.exp(score - new_top[..., None]), 0.0)
    total = jnp.sum(weight, axis=-1)
    accum = jnp.einsum(
        "tkgn,nkd->tkgd",
        weight.astype(jnp.bfloat16),
        value_heads,
        preferred_element_type=jnp.float32,
    )
    top, total, accum = (new_top, total, accum)
    return (
        (accum / total[..., None])
        .astype(jnp.bfloat16)
        .reshape(tok_rows, kv_dev * query_group * HEAD_SIZE)
    )


def expert_work(gate_w, up_w, down_w):

    def work(block):
        gate = jnp.einsum("secd,ehd->sech", block, gate_w, preferred_element_type=jnp.float32)
        up = jnp.einsum("secd,ehd->sech", block, up_w, preferred_element_type=jnp.float32)
        hidden = (jax.nn.silu(gate) * up).astype(jnp.bfloat16)
        wide = lax.all_gather(hidden, "fold", axis=3, tiled=True)
        result = jnp.einsum(
            "sech,ehd->secd", wide, down_w, preferred_element_type=jnp.float32
        ).astype(jnp.bfloat16)
        return lax.all_to_all(result, "cp", split_axis=0, concat_axis=0, tiled=True)

    return work


def body(
    activations,
    queries,
    keys,
    values,
    segments,
    routes,
    route_weight,
    norm_gain,
    w_out,
    w_gate,
    w_up,
    w_down,
):
    resid_in = activations[0]
    segment = segments[0]
    segment_half = segment.astype(jnp.bfloat16)
    chosen = routes[0]
    shares = route_weight[0]
    gain = norm_gain[0]
    proj_local = w_out[0]
    gate_w = w_gate[0]
    up_w = w_up[0]
    down_w = w_down[0]
    tok_rows = resid_in.shape[0]
    cp_count = lax.axis_size("cp")
    attended = attend(queries[0], keys[0], values[0], segment_half)
    partial_sum = jnp.dot(
        attended,
        lax.all_gather(proj_local, "cp", axis=1, tiled=True),
        preferred_element_type=jnp.float32,
    )
    mixed = lax.psum_scatter(partial_sum, "fold", scatter_dimension=1, tiled=True)
    resid = (resid_in.astype(jnp.float32) + mixed).astype(jnp.bfloat16)
    local = resid.astype(jnp.float32)
    exp_dev = gate_w.shape[0]
    experts = exp_dev * cp_count
    top_count = chosen.shape[1]
    capacity = capacity_of(tok_rows, top_count, experts)
    places = slot_places(chosen, experts, capacity)
    work = expert_work(gate_w, up_w, down_w)
    whole, gain_all = (
        lax.all_gather(resid, "fold", axis=1, tiled=True),
        lax.all_gather(gain, "fold", axis=0, tiled=True),
    )
    wide = whole.astype(jnp.float32)
    stat = jnp.mean(wide * wide, axis=1, keepdims=True)
    normed = (wide * lax.rsqrt(stat + EPS) * gain_all.astype(jnp.float32)[None, :]).astype(
        jnp.bfloat16
    )
    buffer = (
        jnp.zeros((experts * capacity, normed.shape[1]), jnp.bfloat16)
        .at[places]
        .set(jnp.repeat(normed, top_count, axis=0))
    )
    outgoing = buffer.reshape(cp_count, exp_dev, capacity, normed.shape[1])
    returned = work(lax.all_to_all(outgoing, "cp", split_axis=0, concat_axis=0, tiled=True))
    results = returned.reshape(experts * capacity, returned.shape[3])
    picked = results[places].reshape(tok_rows, top_count, results.shape[1]).astype(jnp.float32)
    moe = jnp.sum(shares[:, :, None] * picked, axis=1)
    layer_out = (local + moe).astype(jnp.bfloat16)
    moved, moved_segments = shifted((layer_out[None], segment_half[None]), "section", 1)
    return (moved, moved_segments.astype(jnp.int32))


def solution(mesh):
    return jax.shard_map(
        body,
        mesh=mesh,
        in_specs=(
            P("section", "cp", "fold"),
            P("section", "cp", "fold"),
            P("section", "cp", "fold"),
            P("section", "cp", "fold"),
            P("section", "cp"),
            P("section", "cp", None),
            P("section", "cp", None),
            P("section", "fold"),
            P("section", "fold", "cp"),
            P("section", "cp", "fold", None),
            P("section", "cp", "fold", None),
            P("section", "cp", None, "fold"),
        ),
        out_specs=(P("section", "cp", "fold"), P("section", "cp")),
        check_vma=False,
    )
```

profile of v0, /device:TPU:32, one launch (start us, length us, event | category | flops | bytes accessed | tf_op | source)
XLA Modules:
  0.0 844.8 jit_solution(9145623483380738504)
XLA Ops:
  12.1 33.9 %all-gather = bf16[1,4096]{1,0:T(2,128)(2,1)S(1)} all-gather(bf16[1,128]{1,0:T(2,128)(2,1)S(1)} %get-tuple-element.2), channel_id=2, replica_groups=mesh['section'=2,'cp'=32,'fold'=4] {'cp'}, dimensions={1}, use_global_device_ids=true | all-gather | bytes 8448 | tf_op jit(solution)/shard_map/all_gather | solution.py:42
  47.4 27.8 %all-gather.15.cloned.1.call-done = bf16[1,4096,128]{2,1,0:T(8,128)(2,1)} async-done(((bf16[1,128,128]{2,1,0:T(8,128)(2,1)}), bf16[1,4096,128]{2,1,0:T(8,128)(2,1)}) %all-gather.15.cloned.1.call-update) | async-done | bytes 1048592 | tf_op jit(solution)/shard_map/all_gather | solution.py:40
  75.2 3.9 fusion
  79.2 5.7 copy-done.1
  84.9 4.0 fusion.5
  88.9 51.5 %all-gather.17.cloned.1.call-done = bf16[1,4096,128]{1,2,0:T(8,128)(2,1)} async-done(((bf16[1,128,128]{1,2,0:T(8,128)(2,1)}), bf16[1,4096,128]{1,2,0:T(8,128)(2,1)}) %all-gather.17.cloned.1.call-update) | async-done | bytes 1048592 | tf_op jit(solution)/shard_map/all_gather | solution.py:41
  140.4 10.2 %fusion.50 = bf16[1,128,128,8]{2,1,3,0:T(8,128)(2,1)S(1)} fusion(f32[4096,128,8]{1,0,2:T(8,128)} %copy-done.1, f32[128,8]{0,1:T(8,128)S(1)} %broadcast_maximum_fusion, pred[128,4096]{0,1:T(8,128)(4,1)} %fusion.26, bf16[1,4096,128]{1,2,0:T(8,128)(2,1)} %all-gather.17.cloned.1.call-done, f32[128,8]{0,1:T(8,128)S(1)} %fusion.5), kind=kOutput, calls=%fused_computation.47 | convolution fusion | flops 1094975488 | bytes 18620416 | tf_op jit(solution)/shard_map/tkgn,nkd->tkgd/dot_general | solution.py:56
  150.6 79.2 %all-gather.19.cloned.1.call-done = bf16[1,1024,4096]{2,1,0:T(8,128)(2,1)} async-done(((bf16[1,1024,128]{2,1,0:T(8,128)(2,1)}), bf16[1,1024,4096]{2,1,0:T(8,128)(2,1)}) %all-gather.19.cloned.1.call-update) | async-done | bytes 8388624 | tf_op jit(solution)/shard_map/all_gather | solution.py:114
  229.9 6.0 fusion.10
  236.0 30.9 %reduce-scatter.2.cloned.1.call-done = f32[128,1024]{1,0:T(8,128)} async-done(((f32[128,4096]{1,0:T(8,128)}), f32[128,1024]{1,0:T(8,128)}) %reduce-scatter.2.cloned.1.call-update) | async-done | bytes 524304 | tf_op jit(solution)/shard_map/reduce_scatter | solution.py:117
  266.9 1.9 fusion.55
  269.1 12.1 %all-gather.4 = bf16[1,4096]{1,0:T(2,128)(2,1)S(1)} all-gather(bf16[1,1024]{1,0:T(2,128)(2,1)S(1)} %copy-done.5), channel_id=6, replica_groups=mesh['section'=2,'cp'=32,'fold'=4] {'fold'}, dimensions={1}, use_global_device_ids=true | all-gather | bytes 10240 | tf_op jit(solution)/shard_map/all_gather | solution.py:128
  282.0 31.1 %reduce-window.6 = s32[64,8,128]{2,1,0:T(8,128)S(1)} reduce-window(s32[64,8,128]{2,1,0:T(8,128)} %fusion.60, s32[]{:T(128)} %constant.14.clone.1), window={size=1x1x128 pad=0_0x0_0x127_0}, to_apply=%region_3.4 | reduce-window | flops 8323072 | bytes 524292 | tf_op jit(solution)/shard_map/reduce-window
  317.1 2.5 fusion.25
  319.6 17.8 %scatter_custom_fusion = bf16[1280,4096]{1,0:T(8,128)(2,1)} fusion(s32[1024]{0:T(1024)S(1)} %bitcast.141, bf16[]{:T(256)} %constant.12.clone.1, bf16[128,4096]{1,0:T(8,128)(2,1)} %fusion.25), kind=kCustom, calls=%fused_computation.12 | custom fusion | bytes 11534338 | tf_op jit(solution)/shard_map/scatter | solution.py:138
  337.4 14.0 %reshape.167 = bf16[32,2,20,4096]{3,2,1,0:T(8,128)(2,1)} reshape(bf16[1280,4096]{1,0:T(8,128)(2,1)} %scatter_custom_fusion) | data formatting | bytes 20971520 | tf_op jit(solution)/shard_map/reshape | solution.py:140
  351.4 18.6 %copy.52 = bf16[32,2,20,4096]{3,1,2,0:T(2,128)(2,1)S(1)} copy(bf16[32,2,20,4096]{3,2,1,0:T(8,128)(2,1)} %reshape.167) | data formatting | bytes 20971520 | tf_op jit(solution)/shard_map/reshape | solution.py:140
  370.0 239.9 %all_to_all.10 = bf16[32,2,20,4096]{3,1,2,0:T(2,128)(2,1)} all-to-all(bf16[32,2,20,4096]{3,1,2,0:T(2,128)(2,1)S(1)} %copy.52), channel_id=1, replica_groups=mesh['section'=2,'cp'=32,'fold'=4] {'cp'}, dimensions={0} | all-to-all | bytes 20971520 | tf_op jit(solution)/shard_map/all_to_all | solution.py:141
  610.0 14.0 %fusion.3 = f32[2,32,20,192]{3,2,1,0:T(8,128)S(1)} fusion(bf16[32,2,20,4096]{3,1,2,0:T(2,128)(2,1)} %all_to_all.10, bf16[1,2,192,4096]{3,2,1,0:T(8,128)(2,1)S(1)} %copy-done.7), kind=kOutput, calls=%fused_computation.7 | convolution fusion | flops 2013265920 | bytes 14614528 | tf_op jit(solution)/shard_map/secd,ehd->sech/dot_general | solution.py:73
  624.0 13.9 %fusion.31 = bf16[32,2,20,192]{3,2,0,1:T(8,128)(2,1)} fusion(f32[2,32,20,192]{3,2,1,0:T(8,128)S(1)} %fusion.3, bf16[1,2,192,4096]{3,2,1,0:T(8,128)(2,1)} %param.22, bf16[32,2,20,4096]{3,1,2,0:T(2,128)(2,1)} %all_to_all.10), kind=kOutput, calls=%fused_computation.36 | convolution fusion | flops 2014740480 | bytes 15106048 | tf_op jit(solution)/shard_map/secd,ehd->sech/dot_general | solution.py:74
  637.9 5.8 copy.55
  643.8 76.8 %all-gather.13.cloned.1.call-done = bf16[32,2,20,768]{0,1,2,3:T(2,128)(2,1)} async-done(((bf16[32,2,20,192]{0,1,2,3:T(2,128)(2,1)}), bf16[32,2,20,768]{0,1,2,3:T(2,128)(2,1)}) %all-gather.13.cloned.1.call-update) | async-done | bytes 1966096 | tf_op jit(solution)/shard_map/all_gather | solution.py:76
  720.6 11.3 %convert_bitcast_fusion = bf16[32,2,20,1024]{3,0,2,1:T(8,128)(2,1)S(1)} fusion(bf16[1,2,768,1024]{3,2,1,0:T(8,128)(2,1)S(1)} %copy-done, bf16[32,2,20,768]{0,1,2,3:T(2,128)(2,1)} %all-gather.13.cloned.1.call-done), kind=kOutput, calls=%fused_computation.29 | convolution fusion | flops 2014576640 | bytes 7733248 | tf_op jit(solution)/shard_map/sech,ehd->secd/dot_general | solution.py:77
  731.9 4.2 copy.57
  736.1 8.6 %all-to-all-start.1 = ((bf16[32,2,20,1024]{3,1,2,0:T(2,128)(2,1)}), bf16[32,2,20,1024]{3,1,2,0:T(2,128)(2,1)}, u32[]{:S(2)}, u32[]{:S(2)}) async-start(bf16[32,2,20,1024]{3,1,2,0:T(2,128)(2,1)} %copy.57), calls=%async_computation.2 | async-start | bytes 5242880 | tf_op jit(solution)/shard_map/all_to_all | solution.py:80
  744.8 61.6 %all-to-all-done.1 = bf16[32,2,20,1024]{3,1,2,0:T(2,128)(2,1)} async-done(((bf16[32,2,20,1024]{3,1,2,0:T(2,128)(2,1)}), bf16[32,2,20,1024]{3,1,2,0:T(2,128)(2,1)}, u32[]{:S(2)}, u32[]{:S(2)}) %all-to-all-start.1) | async-done | bytes 2621472 | tf_op jit(solution)/shard_map/all_to_all | solution.py:80
  806.4 4.3 copy.58
  810.7 5.2 reshape.168
  815.9 8.1 gather_fusion
  824.1 2.9 fusion.18
  827.1 2.8 collective-permute-start
  830.7 5.9 collective-permute-done.1
  (60 shorter events, 13.7 us)
Async XLA Ops:
  7.2 713.4 %copy-start = (bf16[1,2,768,1024]{3,2,1,0:T(8,128)(2,1)S(1)}, bf16[1,2,768,1024]{3,2,1,0:T(8,128)(2,1)}, u32[]{:S(2)}) copy-start(bf16[1,2,768,1024]{3,2,1,0:T(8,128)(2,1)} %param.23) | copy-start | bytes 9437188
  7.2 68.0 %all-gather.15.cloned.1.call-start = ((), (), s32[]{:S(2)}) async-start(), calls=%async_computation.6 | async-start | bytes 1081344 | tf_op jit(solution)/shard_map/all_gather | solution.py:40
  7.9 132.5 %all-gather.17.cloned.1.call-start = ((), (), s32[]{:S(2)}) async-start(), calls=%async_computation.7 | async-start | bytes 1081344 | tf_op jit(solution)/shard_map/all_gather | solution.py:41
  9.6 220.3 %all-gather.19.cloned.1.call-start = ((), (), s32[]{:S(2)}) async-start(), calls=%async_computation.8 | async-start | bytes 8650752 | tf_op jit(solution)/shard_map/all_gather | solution.py:114
  10.4 256.5 %reduce-scatter.2.cloned.1.call-start = ((), (), s32[]{:S(2)}) async-start(), calls=%async_computation.3 | async-start | bytes 2621440 | tf_op jit(solution)/shard_map/reduce_scatter | solution.py:117
  75.2 9.7 %copy-start.2 = (pred[128,4096]{0,1:T(8,128)(4,1)S(1)}, pred[128,4096]{0,1:T(8,128)(4,1)}, u32[]{:S(2)}) copy-start(pred[128,4096]{0,1:T(8,128)(4,1)} %fusion.26) | copy-start | bytes 1572868
  79.2 5.7 copy-start.1
  229.9 38.9 %copy-start.4 = (s32[1,128,8]{1,2,0:T(8,128)S(1)}, s32[1,128,8]{1,2,0:T(8,128)}, u32[]{:S(2)}) copy-start(s32[1,128,8]{1,2,0:T(8,128)} %param.17) | copy-start | bytes 12292
  229.9 39.2 %copy-start.5 = (bf16[1,1024]{1,0:T(2,128)(2,1)S(1)}, bf16[1,1024]{1,0:T(2,128)(2,1)}, u32[]{:S(2)}) copy-start(bf16[1,1024]{1,0:T(2,128)(2,1)} %param.19) | copy-start | bytes 6148
  235.9 79.6 %all-gather.11.cloned.1.call-start = ((), (), s32[]{:S(2)}) async-start(), calls=%async_computation.4 | async-start | bytes 1310720 | tf_op jit(solution)/shard_map/all_gather | solution.py:127
  268.8 451.8 %all-gather.13.cloned.1.call-start = ((), (), s32[]{:S(2)}) async-start(), calls=%async_computation.5 | async-start | bytes 9830400 | tf_op jit(solution)/shard_map/all_gather | solution.py:76
  370.0 239.9 %copy-start.7 = (bf16[1,2,192,4096]{3,2,1,0:T(8,128)(2,1)S(1)}, bf16[1,2,192,4096]{3,2,1,0:T(8,128)(2,1)}, u32[]{:S(2)}) copy-start(bf16[1,2,192,4096]{3,2,1,0:T(8,128)(2,1)} %param.21) | copy-start | bytes 9437188
  731.9 12.8 %copy-start.6 = (f32[1,128,8]{1,2,0:T(8,128)S(1)}, f32[1,128,8]{1,2,0:T(8,128)}, u32[]{:S(2)}) copy-start(f32[1,128,8]{1,2,0:T(8,128)} %param.18) | copy-start | bytes 12292
  736.1 70.3 %all-to-all-start.1 = ((bf16[32,2,20,1024]{3,1,2,0:T(2,128)(2,1)}), bf16[32,2,20,1024]{3,1,2,0:T(2,128)(2,1)}, u32[]{:S(2)}, u32[]{:S(2)}) async-start(bf16[32,2,20,1024]{3,1,2,0:T(2,128)(2,1)} %copy.57), calls=%async_computation.2 | async-start | bytes 5242880 | tf_op jit(solution)/shard_map/all_to_all | solution.py:80
  815.9 11.1 %copy-start.3 = (bf16[128,1024]{1,0:T(8,128)(2,1)S(1)}, bf16[128,1024]{1,0:T(8,128)(2,1)}, u32[]{:S(2)}) copy-start(bf16[128,1024]{1,0:T(8,128)(2,1)} %fusion.55) | copy-start | bytes 786436
  827.1 10.0 %collective-permute-start = (bf16[1,128,1024]{2,1,0:T(8,128)(2,1)S(1)}, bf16[1,128,1024]{2,1,0:T(8,128)(2,1)S(1)}, u32[]{:S(2)}, u32[]{:S(2)}) collective-permute-start(bf16[1,128,1024]{2,1,0:T(8,128)(2,1)S(1)} %fusion.56), channel_id=1, source_target_pairs={{0,128},{128,0},{1,129},{129,1},{2,130},{130,2},{3,131},{131,3},{4... | collective-permute-start | bytes 786440 | tf_op jit(solution)/shard_map/ppermute | solution.py:17
  829.8 6.7 collective-permute-start.1
Sparse Core Ops, SparseCore 0:
  9.9 65.3 all-gather.14
  77.6 62.8 all-gather.16
  142.2 87.6 all-gather.18
  236.1 30.7 reduce-scatter.1
  268.9 26.2 all-gather.10
  643.9 76.6 all-gather.12
where the time goes:
time: 854 us; the launch traced here: 845 us
  waiting for transfers between devices  335 us (39%)
  blocking collectives  286 us (33%)
  local copies, waits for them, and re-layouts  89.7 us (11%)
  matrix products  59.4 us (7%)
  other arithmetic  47.7 us (6%)
  between operations  14.5 us (2%)
  starting transfers between devices  12.4 us (1%)
    all_to_all x1, blocking collectives, body(): lax.all_to_all(outgoing, 'cp', split_axis=0, concat_axis=0, tiled=True)  240 us
    all_gather x1, waiting for transfers between devices, body(): lax.all_gather(proj_local, 'cp', axis=1, tiled=True)  79.2 us
    all_gather x1, waiting for transfers between devices, work(): wide = lax.all_gather(hidden, 'fold', axis=3, tiled=True)  76.8 us
    all_to_all x1, waiting for transfers between devices, work(): return lax.all_to_all(result, 'cp', split_axis=0, concat_axis=0, tiled=True)  61.6 us
    all_gather x1, waiting for transfers between devices, attend(): v_piece = lax.all_gather(values, 'cp', axis=0, tiled=True)  51.5 us
    all_gather x1, blocking collectives, attend(): s_piece = lax.all_gather(segment, 'cp', axis=0, tiled=True)  33.9 us
    reshape x2, local copies, waits for them, and re-layouts, body(): outgoing = buffer.reshape(cp_count, exp_dev, capacity, normed.shape[1])  32.6 us
    another operation x2, other arithmetic  31.1 us
  transfers between devices with their start and end apart: 9, of which 7 were waited for; matrix products, arithmetic and copies ran while one was open for 7% of the time, Pallas kernels for 0%

commit v1 on v0

v1 whole, which is shorter than its diff:
```python
import functools
import math

import jax
import jax.numpy as jnp
from jax import lax
from jax.experimental import pallas as pl
from jax.experimental.pallas import tpu as pltpu
from jax.sharding import PartitionSpec as P

MESH = pl.DeviceIdType.MESH
HEAD = 128
NZ = 8
FOLD = 4
NEG = -1e30
EPS = 1e-06
CAP = 20
F32 = jnp.float32
BF16 = jnp.bfloat16


def place(x, z, c):
    return x * (2 * NZ) + lax.rem(z + 2 * NZ, NZ) * 2 + c


class Net:
    def __init__(self, send, recv):
        self.send_sems, self.recv_sems = send, recv
        cp = lax.axis_index("cp")
        self.cp = cp
        self.x = cp // (2 * NZ)
        self.z = (cp // 2) % NZ
        self.c = cp % 2
        self.f = lax.axis_index("fold")
        self.xp = 1 - self.x
        self.fp, self.fo, self.fm = [lax.rem(self.f + k, FOLD) for k in (1, 2, 3)]
        self.ids = {}
        self.sent = []

    def to(self, way):
        x, z, c = self.x, self.z, self.c
        if way == "z+":
            return {"cp": place(x, z + 1, c)}
        if way == "z-":
            return {"cp": place(x, z - 1, c)}
        if way == "x":
            return {"cp": place(1 - x, z, c)}
        if way == "c":
            return {"cp": place(x, z, 1 - c)}
        if way == "f+":
            return {"fold": self.fp}
        if way == "f-":
            return {"fold": self.fm}
        if way == "fo":
            return {"fold": self.fo}
        return {"section": 1 - lax.axis_index("section")}

    def barrier(self, ways):
        sem = pltpu.get_barrier_semaphore()
        for way in ways:
            pl.semaphore_signal(sem, inc=1, device_id=self.to(way), device_id_type=MESH)
        pl.semaphore_wait(sem, len(ways))

    def slot(self, name):
        return self.ids.setdefault(name, len(self.ids))

    def copy(self, name, src, dst, way):
        i = self.slot(name)
        return pltpu.make_async_remote_copy(
            src_ref=src,
            dst_ref=dst,
            send_sem=self.send_sems.at[i],
            recv_sem=self.recv_sems.at[i],
            device_id=self.to(way),
            device_id_type=MESH,
        )

    def push(self, name, src, dst, way):
        copy = self.copy(name, src, dst, way)
        copy.start()
        self.sent.append(copy)

    def await_(self, name, dst, way):
        self.copy(name, dst, dst, way).wait_recv()

    def finish(self):
        for copy in self.sent:
            copy.wait_send()


class Gather:
    def __init__(self, net, name, buf, own, rows1):
        self.net, self.name, self.buf, self.own = net, name, buf, own
        self.rows = buf.shape[1]
        self.rows1 = rows1

    def block(self, x, z, c, part="full"):
        ref = self.buf.at[place(x, z, c)]
        if part == "full":
            return ref
        if part == "r1":
            return ref.at[pl.ds(0, self.rows1)]
        return ref.at[pl.ds(self.rows1, self.rows - self.rows1)]

    def push(self, tag, key, way, part="full", src=None):
        ref = self.block(*key, part)
        self.net.push((self.name, tag), ref if src is None else src, ref, way)

    def wait(self, tag, key, way, part="full"):
        self.net.await_((self.name, tag), self.block(*key, part), way)

    def tick(self, s):
        n = self.net
        x, z, c, xp, cp = n.x, n.z, n.c, n.xp, 1 - n.c
        if s == 0:
            for tag, way in (("zp0", "z+"), ("zm0", "z-"), ("x0", "x"), ("c0", "c")):
                self.push(tag, (x, z, c), way, src=self.own)
            return
        if s == 1:
            self.wait("x0", (xp, z, c), "x")
            self.push("yp0", (xp, z, c), "z+", "r2")
            self.push("ym0", (xp, z, c), "z-", "r2")
            self.push("cx0", (xp, z, c), "c")
        if s <= 4:
            self.wait(f"zp{s - 1}", (x, z - s, c), "z+")
            if s <= 3:
                self.push(f"zp{s}", (x, z - s, c), "z+")
                self.wait(f"zm{s - 1}", (x, z + s, c), "z-")
                if s <= 2:
                    self.push(f"zm{s}", (x, z + s, c), "z-")
            self.push(f"xm{s}", (x, z - s, c), "x", "r1")
            if s <= 3:
                self.push(f"xp{s}", (x, z + s, c), "x", "r1")
            self.push(f"cm{s}", (x, z - s, c), "c")
            if s <= 3:
                self.push(f"cp{s}", (x, z + s, c), "c")
        if s >= 2 and s <= 5:
            d = s - 1
            self.wait(f"ym{d - 1}", (xp, z + d, c), "z-", "r2")
            if d <= 3:
                self.push(f"ym{d}", (xp, z + d, c), "z-", "r2")
                self.wait(f"yp{d - 1}", (xp, z - d, c), "z+", "r2")
                if d <= 2:
                    self.push(f"yp{d}", (xp, z - d, c), "z+", "r2")
            self.push(f"dp{d}", (xp, z + d, c), "c", "r2")
            if d <= 3:
                self.push(f"dm{d}", (xp, z - d, c), "c", "r2")
            self.wait(f"xm{d}", (xp, z - d, c), "x", "r1")
            self.push(f"em{d}", (xp, z - d, c), "c", "r1")
            if d <= 3:
                self.wait(f"xp{d}", (xp, z + d, c), "x", "r1")
                self.push(f"ep{d}", (xp, z + d, c), "c", "r1")

    def ready(self, d):
        n = self.net
        x, z, xp, cp = n.x, n.z, n.xp, 1 - n.c
        if d == 0:
            self.wait("c0", (x, z, cp), "c")
            self.wait("cx0", (xp, z, cp), "c")
            return
        side, s = ("p", d) if d > 0 else ("m", -d)
        self.wait(f"c{side}{s}", (x, z + d, cp), "c")
        self.wait(f"d{'p' if s == 4 else side}{s}", (xp, z + d, cp), "c", "r2")
        self.wait(f"e{side}{s}", (xp, z + d, cp), "c", "r1")


DISTANCES = (0, -1, 1, -2, 2, -3, 3, -4)


def front(
    q, kvm, segq, act, gain, wo, wg, wu,
    resid, normed, rank, share, wg_out, wu_out,
    kvg, wog, bias, attended, hits, part, ra, rb, rc, rd, stat, send, recv, local,
):
    net = Net(send, recv)
    f, fp, fo, fm = net.f, net.fp, net.fo, net.fm
    tokens = q.shape[0]
    hid = wg.shape[1]
    feats = wg_out.shape[2]
    heads = q.shape[1] // HEAD
    net.barrier(("z+", "z-", "x", "c", "f+", "f-", "fo"))

    kv = Gather(net, "kv", kvg, kvm, kvm.shape[0] * 3 // 5)
    out = Gather(net, "wo", wog, wo, wo.shape[0] * 5 // 8)
    kv.tick(0)
    out.tick(0)
    kvg[net.cp] = kvm[...]
    keep = [pltpu.make_async_copy(wo, wog.at[net.cp], local.at[0])]
    for k, (src, dst) in enumerate(((wg, wg_out), (wu, wu_out))):
        rows = pl.ds(f * hid, hid)
        for way, t in (("f+", fp), ("f-", fm), ("fo", fo)):
            net.push(("w", k, way), src.at[:, :, pl.ds(t * feats, feats)], dst.at[:, rows, :], way)
        keep.append(
            pltpu.make_async_copy(src.at[:, :, pl.ds(f * feats, feats)], dst.at[:, rows, :], local.at[k + 1])
        )
    for copy in keep:
        copy.start()

    for s in range(1, 6):
        kv.tick(s)
        if s == 4:
            out.tick(1)
    for d in DISTANCES:
        kv.ready(d)
    out.tick(2)

    window = 17
    start = jnp.maximum(net.cp - (window - 1), 0)
    span = window * tokens
    seg_k = jnp.concatenate(
        [kvg[start + i, tokens:tokens + 16, HEAD:2 * HEAD].astype(F32)[0:1] for i in range(window)], axis=1
    )
    q_place = net.cp * tokens + lax.broadcasted_iota(jnp.int32, (tokens, span), 0)
    k_place = start * tokens + lax.broadcasted_iota(jnp.int32, (tokens, span), 1)
    allowed = (k_place <= q_place) & (seg_k == segq[:, 0:1])
    bias[...] = jnp.where(allowed, 0.0, NEG)
    factor = math.log2(math.e) / math.sqrt(HEAD)

    def head(h, carry):
        columns = pl.ds(pl.multiple_of(h * HEAD, HEAD), HEAD)
        keys = kvg[pl.ds(start, window), 0:tokens, 0:HEAD].reshape(span, HEAD)
        vals = kvg[pl.ds(start, window), 0:tokens, HEAD:2 * HEAD].reshape(span, HEAD)
        score = lax.dot_general(q[:, columns], keys, (((1,), (1,)), ((), ())), preferred_element_type=F32)
        score = score * factor + bias[...]
        top = jnp.max(score, axis=1, keepdims=True)
        weight = jnp.exp2(score - top)
        total = jnp.sum(weight, axis=1, keepdims=True)
        mixed = jnp.dot(weight.astype(BF16), vals, preferred_element_type=F32)
        attended[:, columns] = (mixed / total).astype(BF16)
        return carry

    lax.fori_loop(0, heads // 2, head, 0)
    out.tick(3)
    lax.fori_loop(heads // 2, heads, head, 0)

    for g in range(NZ):
        for e in range(2):
            expert = (2 * net.cp + e).astype(F32)
            for k in range(4):
                block = place(k // 2, g, k % 2)
                meta = kvg[block, tokens:tokens + 32, 0:tokens].astype(F32)
                chosen = meta[0:8] == expert
                row = pl.ds(2 * g + e, 1)
                columns = pl.ds(k * tokens, tokens)
                hits[row, columns] = jnp.sum(jnp.where(chosen, 1.0, 0.0), axis=0, keepdims=True)
                shares = meta[8:16] + meta[16:24] + meta[24:32]
                share[row, columns] = jnp.sum(jnp.where(chosen, shares, 0.0), axis=0, keepdims=True)
    out.tick(4)
    wide = 4 * tokens
    earlier = lax.broadcasted_iota(jnp.int32, (wide, wide), 0) < lax.broadcasted_iota(jnp.int32, (wide, wide), 1)
    hit = hits[...]
    before = jnp.dot(hit.astype(BF16), jnp.where(earlier, 1.0, 0.0).astype(BF16), preferred_element_type=F32)
    rank[...] = jnp.where(hit > 0.5, before, -1.0)
    out.tick(5)
    for d in DISTANCES:
        out.ready(d)
    keep[0].wait()

    per = 2 * NZ * 2 // FOLD
    cut = wo.shape[1]

    def project(t):
        lhs = attended[...]
        for i in range(per):
            part[t, :, i * cut:(i + 1) * cut] = jnp.dot(
                lhs, wog[t * per + i], preferred_element_type=F32
            ).astype(BF16)

    half = feats // 2
    project(fo)
    net.push("pa", part.at[fo, :, pl.ds(0, half)], ra, "f+")
    net.push("pb", part.at[fo, :, pl.ds(half, half)], rb, "f-")
    project(fp)
    project(fm)
    net.await_("pa", ra, "f+")
    part[fp, :, 0:half] = (part[fp, :, 0:half].astype(F32) + ra[...].astype(F32)).astype(BF16)
    net.push("pc", part.at[fp], rc, "f+")
    net.await_("pb", rb, "f-")
    part[fm, :, half:2 * half] = (part[fm, :, half:2 * half].astype(F32) + rb[...].astype(F32)).astype(BF16)
    net.push("pd", part.at[fm], rd, "f-")
    project(f)
    base = act[...].astype(F32) + part[f].astype(F32)
    net.await_("pc", rc, "f+")
    net.await_("pd", rd, "f-")
    kept = (base + rc[...].astype(F32) + rd[...].astype(F32)).astype(BF16)
    resid[...] = kept
    local_wide = kept.astype(F32)
    squares = jnp.sum(local_wide * local_wide, axis=1, keepdims=True)
    stat[0] = jnp.broadcast_to(squares, stat.shape[1:])
    for k, way in enumerate(("f+", "f-", "fo")):
        net.push(("s", k), stat.at[0], stat.at[k + 1], way)
    for k, way in enumerate(("f+", "f-", "fo")):
        net.await_(("s", k), stat.at[k + 1], way)
    total = (stat[0] + stat[1] + stat[2] + stat[3])[:, 0:1]
    scale = lax.rsqrt(total / (feats * FOLD) + EPS)
    normed[...] = (local_wide * scale * gain[...].astype(F32)).astype(BF16)

    for k, dst in enumerate((wg_out, wu_out)):
        for way, t in (("f+", fm), ("f-", fp), ("fo", fo)):
            net.await_(("w", k, way), dst.at[:, pl.ds(t * hid, hid), :], way)
        keep[k + 1].wait()
    net.finish()


STAGES = ((0, -1), (1, -2), (2, -3), (3, -4))


def back(
    xn, resid, rank, share, wg, wu, wd,
    passed,
    xg, wgv, wuv, wdv, slots, part, ra, rb, rc, rd, hidden, ysum, cin, xin, zin, yin, tin, result,
    send, recv, local,
):
    net = Net(send, recv)
    x, z, c, xp, cpeer = net.x, net.z, net.c, net.xp, 1 - net.c
    f, fp, fo, fm = net.f, net.fp, net.fo, net.fm
    tokens = xn.shape[0]
    hid = wgv.shape[1]
    cap = part.shape[2]
    net.barrier(("z+", "z-", "x", "c", "f+", "f-", "sec"))
    rows1 = tokens * 5 // 8
    rows2 = tokens - rows1
    xs = Gather(net, "x", xg, xn, rows1)
    xs.tick(0)
    loads = [
        pltpu.make_async_copy(src, dst, local.at[k]) for k, (src, dst) in enumerate(((wg, wgv), (wu, wuv), (wd, wdv)))
    ]
    for copy in loads:
        copy.start()
    xg[net.cp] = xn[...]

    def group(d):
        return lax.rem(z + d + NZ, NZ)

    def pick(d, e):
        row = rank[pl.ds(2 * group(d) + e, 1), :]
        want = lax.broadcasted_iota(jnp.int32, (cap, 4 * tokens), 0).astype(F32)
        return jnp.where(want == row, 1.0, 0.0)

    def enter(i):
        for j, d in enumerate(STAGES[i]):
            xs.ready(d)
            g = group(d)
            low = xg[pl.ds(2 * g, 2)].reshape(2 * tokens, xn.shape[1])
            high = xg[pl.ds(2 * NZ + 2 * g, 2)].reshape(2 * tokens, xn.shape[1])
            choice = jnp.concatenate([pick(d, 0), pick(d, 1)], axis=0).astype(BF16)
            got = jnp.dot(choice[:, 0:2 * tokens], low, preferred_element_type=F32)
            got = (got + jnp.dot(choice[:, 2 * tokens:], high, preferred_element_type=F32)).astype(BF16)
            for e in range(2):
                slots[pl.ds((2 * e + j) * cap, cap), :] = got[e * cap:(e + 1) * cap]
        for e in range(2):
            lhs = slots[pl.ds(2 * e * cap, 2 * cap), :]
            for k, w in enumerate((wgv, wuv)):
                out = lax.dot_general(lhs, w[e], (((1,), (1,)), ((), ())), preferred_element_type=F32).astype(BF16)
                part[i, 2 * e, :, k * hid:(k + 1) * hid] = out[0:cap]
                part[i, 2 * e + 1, :, k * hid:(k + 1) * hid] = out[cap:]
        net.push(("a", i), part.at[i, fo, :, pl.ds(0, hid)], ra.at[i], "f+")
        net.push(("b", i), part.at[i, fo, :, pl.ds(hid, hid)], rb.at[i], "f-")

    def relay(i):
        net.await_(("a", i), ra.at[i], "f+")
        part[i, fp, :, 0:hid] = (part[i, fp, :, 0:hid].astype(F32) + ra[i].astype(F32)).astype(BF16)
        net.push(("c", i), part.at[i, fp], rc.at[i], "f+")
        net.await_(("b", i), rb.at[i], "f-")
        part[i, fm, :, hid:2 * hid] = (part[i, fm, :, hid:2 * hid].astype(F32) + rb[i].astype(F32)).astype(BF16)
        net.push(("d", i), part.at[i, fm], rd.at[i], "f-")

    def activate(i):
        net.await_(("c", i), rc.at[i], "f+")
        net.await_(("d", i), rd.at[i], "f-")
        total = part[i, f].astype(F32) + rc[i].astype(F32) + rd[i].astype(F32)
        gate, up = total[:, 0:hid], total[:, hid:2 * hid]
        hidden[i, f] = (gate / (1.0 + jnp.exp(-gate)) * up).astype(BF16)
        net.push(("h+", i), hidden.at[i, f], hidden.at[i, f], "f+")
        net.push(("h-", i), hidden.at[i, f], hidden.at[i, f], "f-")

    def spread(i):
        half = hid // 2
        net.await_(("h+", i), hidden.at[i, fm], "f+")
        lower = hidden.at[i, fm, :, pl.ds(0, half)]
        net.push(("i+", i), lower, lower, "f+")
        net.await_(("h-", i), hidden.at[i, fp], "f-")
        upper = hidden.at[i, fp, :, pl.ds(half, half)]
        net.push(("i-", i), upper, upper, "f-")

    def leave(i):
        half = hid // 2
        net.await_(("i+", i), hidden.at[i, fo, :, pl.ds(0, half)], "f+")
        net.await_(("i-", i), hidden.at[i, fo, :, pl.ds(half, half)], "f-")
        for e in range(2):
            lhs = hidden[i, 2 * e:2 * e + 2].reshape(2 * cap, hid)
            res = jnp.dot(lhs, wdv[e], preferred_element_type=F32)
            for j, d in enumerate(STAGES[i]):
                row = share[pl.ds(2 * group(d) + e, 1), :]
                weight = jnp.sum(pick(d, e) * row, axis=1, keepdims=True)
                result[2 * j + e] = (res[j * cap:(j + 1) * cap] * weight).astype(BF16)
        for j, d in enumerate(STAGES[i]):
            g = group(d)
            choice = jnp.concatenate([pick(d, 0), pick(d, 1)], axis=0).astype(BF16)
            res = result[2 * j:2 * j + 2].reshape(2 * cap, result.shape[2])
            total = lax.dot_general(choice, res, (((0,), (0,)), ((), ())), preferred_element_type=F32).astype(BF16)
            for k in range(4):
                ysum[place(k // 2, g, k % 2)] = total[k * tokens:(k + 1) * tokens]
            for xx in range(2):
                net.push(("rc", d, xx), ysum.at[place(xx, g, cpeer)], cin.at[g, xx], "c")

    def accumulate(ref, at, rows, inc):
        ref[at, rows] = (ref[at, rows].astype(F32) + inc.astype(F32)).astype(BF16)

    def merge(i):
        for d in STAGES[i]:
            g = group(d)
            for xx in range(2):
                net.await_(("rc", d, xx), cin.at[g, xx], "c")
                accumulate(ysum, place(xx, g, c), pl.ds(0, tokens), cin[g, xx])
            net.push(("rx", d), ysum.at[place(xp, g, c), pl.ds(0, rows1)], xin.at[g], "x")

    def cross(i):
        for d in STAGES[i]:
            g = group(d)
            net.await_(("rx", d), xin.at[g], "x")
            accumulate(ysum, place(x, g, c), pl.ds(0, rows1), xin[g])

    xs.tick(1)
    xs.tick(2)
    for copy in loads:
        copy.wait()
    enter(0)
    xs.tick(3)
    enter(1)
    relay(0)
    xs.tick(4)
    enter(2)
    relay(1)
    activate(0)
    xs.tick(5)
    enter(3)
    relay(2)
    activate(1)
    spread(0)
    relay(3)
    activate(2)
    spread(1)
    leave(0)
    activate(3)
    spread(2)
    leave(1)
    merge(0)
    spread(3)
    leave(2)
    merge(1)
    cross(0)
    leave(3)
    merge(2)
    cross(1)
    merge(3)
    cross(2)
    cross(3)

    full = pl.ds(0, tokens)
    rest = pl.ds(rows1, rows2)
    lines = (("z-", -1, 4, x, zin, 0, full), ("z+", 1, 3, x, zin, 4, full), ("z-", -1, 3, xp, yin, 0, rest), ("z+", 1, 4, xp, yin, 3, rest))
    for step in range(4):
        for k, (way, sign, hops, line, inbox, first, rows) in enumerate(lines):
            s = step - (4 - hops)
            if s < 0:
                continue
            at = place(line, z + sign * (hops - s), c)
            if s > 0:
                net.await_(("rz", k, s - 1), inbox.at[first + s - 1], way)
                accumulate(ysum, at, rows, inbox[first + s - 1])
            net.push(("rz", k, s), ysum.at[at, rows], inbox.at[first + s], way)
    for k, (way, sign, hops, line, inbox, first, rows) in reversed(tuple(enumerate(lines))):
        net.await_(("rz", k, hops - 1), inbox.at[first + hops - 1], way)
        accumulate(ysum, place(line, z, c), rows, inbox[first + hops - 1])
        if k == 2:
            net.push("rt", ysum.at[place(xp, z, c), rest], tin, "x")
    net.await_("rt", tin, "x")
    moe = ysum[net.cp].astype(F32)
    own = resid[...].astype(F32) + moe
    ahead = own[0:rows1].astype(BF16)
    behind = (own[rows1:] + tin[...].astype(F32)).astype(BF16)
    xg[net.cp, 0:rows1] = ahead
    xg[net.cp, rows1:tokens] = behind
    net.push("out", xg.at[net.cp], passed, "sec")
    net.await_("out", passed, "sec")
    net.finish()


def vmem(count):
    return [pl.BlockSpec(memory_space=pltpu.VMEM)] * count


def anywhere(count):
    return [pl.BlockSpec(memory_space=pl.ANY)] * count


def sized(shape, dtype):
    return jax.ShapeDtypeStruct(shape, dtype)


def run_front(q, kvm, segq, act, gain, wo, wg, wu):
    tokens, feats = act.shape
    blocks = 4 * NZ
    span = 17 * tokens
    experts, hid, wide = wg.shape
    dma = pltpu.SemaphoreType.DMA
    return pl.pallas_call(
        front,
        out_shape=(
            sized((tokens, feats), BF16),
            sized((tokens, feats), BF16),
            sized((2 * NZ, 4 * tokens), F32),
            sized((2 * NZ, 4 * tokens), F32),
            sized((experts, hid * FOLD, wide // FOLD), BF16),
            sized((experts, hid * FOLD, wide // FOLD), BF16),
        ),
        in_specs=vmem(6) + anywhere(2),
        out_specs=tuple(vmem(4) + anywhere(2)),
        scratch_shapes=[
            pltpu.VMEM((blocks,) + kvm.shape, BF16),
            pltpu.VMEM((blocks,) + wo.shape, BF16),
            pltpu.VMEM((tokens, span), F32),
            pltpu.VMEM(q.shape, BF16),
            pltpu.VMEM((2 * NZ, 4 * tokens), F32),
            pltpu.VMEM((FOLD, tokens, feats), BF16),
            pltpu.VMEM((tokens, feats // 2), BF16),
            pltpu.VMEM((tokens, feats // 2), BF16),
            pltpu.VMEM((tokens, feats), BF16),
            pltpu.VMEM((tokens, feats), BF16),
            pltpu.VMEM((4, tokens, 128), F32),
            dma((112,)),
            dma((112,)),
            dma((3,)),
        ],
        compiler_params=pltpu.CompilerParams(collective_id=0, has_side_effects=True, vmem_limit_bytes=56 * 2**20),
        name="front",
    )(q, kvm, segq, act, gain, wo, wg, wu)


def run_back(xn, resid, rank, share, wg, wu, wd):
    tokens, feats = xn.shape
    blocks = 4 * NZ
    hid = wg.shape[1]
    cap = 4 * CAP
    rows1 = tokens * 5 // 8
    dma = pltpu.SemaphoreType.DMA
    return pl.pallas_call(
        back,
        out_shape=sized((tokens, feats), BF16),
        in_specs=vmem(4) + anywhere(3),
        out_specs=vmem(1)[0],
        scratch_shapes=[
            pltpu.VMEM((blocks, tokens, feats), BF16),
            pltpu.VMEM(wg.shape, BF16),
            pltpu.VMEM(wu.shape, BF16),
            pltpu.VMEM(wd.shape, BF16),
            pltpu.VMEM((4 * cap, feats), BF16),
            pltpu.VMEM((4, FOLD, cap, 2 * hid), BF16),
            pltpu.VMEM((4, cap, hid), BF16),
            pltpu.VMEM((4, cap, hid), BF16),
            pltpu.VMEM((4, cap, 2 * hid), BF16),
            pltpu.VMEM((4, cap, 2 * hid), BF16),
            pltpu.VMEM((4, FOLD, cap, hid), BF16),
            pltpu.VMEM((blocks, tokens, feats), BF16),
            pltpu.VMEM((NZ, 2, tokens, feats), BF16),
            pltpu.VMEM((NZ, rows1, feats), BF16),
            pltpu.VMEM((7, tokens, feats), BF16),
            pltpu.VMEM((7, tokens - rows1, feats), BF16),
            pltpu.VMEM((tokens - rows1, feats), BF16),
            pltpu.VMEM((4, cap, feats), BF16),
            dma((144,)),
            dma((144,)),
            dma((3,)),
        ],
        compiler_params=pltpu.CompilerParams(collective_id=1, has_side_effects=True, vmem_limit_bytes=60 * 2**20),
        name="back",
    )(xn, resid, rank, share, wg, wu, wd)


def body(
    activations, queries, keys, values, segments, routes, route_weight, norm_gain, w_out, w_gate, w_up, w_down,
):
    segment = segments[0]
    tokens = segment.shape[0]
    weight = route_weight[0].T
    first = lax.reduce_precision(weight, 8, 7)
    second = lax.reduce_precision(weight - first, 8, 7)
    third = weight - first - second
    meta = jnp.concatenate([routes[0].T.astype(F32), first, second, third], axis=0)
    side = jnp.broadcast_to(segment.astype(F32)[None, :], (32, tokens))
    kvm = jnp.concatenate(
        [
            jnp.concatenate([keys[0], values[0]], axis=1),
            jnp.concatenate([meta, side], axis=1).astype(BF16),
        ],
        axis=0,
    )
    segq = jnp.broadcast_to(segment.astype(F32)[:, None], (tokens, 128))
    resid, normed, rank, share, wg, wu = run_front(
        queries[0], kvm, segq, activations[0], norm_gain, w_out[0], w_gate[0], w_up[0]
    )
    passed = run_back(normed, resid, rank, share, wg, wu, w_down[0])
    moved = lax.ppermute(segments, "section", [(0, 1), (1, 0)])
    return passed[None], moved


def solution(mesh):
    return jax.shard_map(
        body,
        mesh=mesh,
        in_specs=(
            P("section", "cp", "fold"),
            P("section", "cp", "fold"),
            P("section", "cp", "fold"),
            P("section", "cp", "fold"),
            P("section", "cp"),
            P("section", "cp", None),
            P("section", "cp", None),
            P("section", "fold"),
            P("section", "fold", "cp"),
            P("section", "cp", "fold", None),
            P("section", "cp", "fold", None),
            P("section", "cp", None, "fold"),
        ),
        out_specs=(P("section", "cp", "fold"), P("section", "cp")),
        check_vma=False,
    )
```

time: 854 us -> 257 us (0.30)
  waiting for transfers between devices: 335 us -> 0.01 us
  blocking collectives: 286 us -> 0 us
  Pallas kernels: 0 us -> 245 us
  local copies, waits for them, and re-layouts: 89.7 us -> 2.89 us
  matrix products: 59.4 us -> 0 us
  other arithmetic: 47.7 us -> 3.49 us
  between operations: 14.5 us -> 0.66 us
  starting transfers between devices: 12.4 us -> 3.11 us
    pallas_call x0 -> x2, Pallas kernels: none -> 245 us  [the longest x1 153 us: run_back(): pl.pallas_call(back, out_shape=sized((tokens, feats), BF16), in_specs=vme...]
    all_to_all x1 -> x0, blocking collectives: 240 us -> none  [body(): lax.all_to_all(outgoing, 'cp', split_axis=0, concat_axis=0, tiled=True)]
    all_gather x5 -> x0, waiting for transfers between devices: 235 us -> none  [the longest x1 79.2 us: body(): lax.all_gather(proj_local, 'cp', axis=1, tiled=True)]
    all_to_all x1 -> x0, waiting for transfers between devices: 61.6 us -> none  [work(): return lax.all_to_all(result, 'cp', split_axis=0, concat_axis=0, tiled=True)]
    dot_general x6 -> x0, matrix products: 59.4 us -> none  [the longest x1 14 us: work(): jnp.einsum('secd,ehd->sech', block, gate_w, preferred_element_type=jnp.fl...]
    all_gather x2 -> x0, blocking collectives: 46 us -> none  [the longest x1 33.9 us: attend(): s_piece = lax.all_gather(segment, 'cp', axis=0, tiled=True)]
    reshape x3 -> x0, local copies, waits for them, and re-layouts: 37.8 us -> none  [the longest x2 32.6 us: body(): outgoing = buffer.reshape(cp_count, exp_dev, capacity, normed.shape[1])]
    reduce_scatter x1 -> x0, waiting for transfers between devices: 30.9 us -> none  [body(): lax.psum_scatter(partial_sum, 'fold', scatter_dimension=1, tiled=True)]
  transfers between devices with their start and end apart: 9 -> 1, of which waited for: 7 -> 0; matrix products, arithmetic and copies ran while one was open for 7% -> 2% of each run, Pallas kernels for 0% -> 96%
where the time goes in v1:
time: 257 us; the launch traced here: 256 us
  Pallas kernels  245 us (95%)
  other arithmetic  3.49 us (1%)
  starting transfers between devices  3.11 us (1%)
  local copies, waits for them, and re-layouts  2.89 us (1%)
    pallas_call x1, Pallas kernels, run_back(): pl.pallas_call(back, out_shape=sized((tokens, feats), BF16), in_specs=vme...  153 us
    pallas_call x1, Pallas kernels, run_front(): pl.pallas_call(front, out_shape=(sized((tokens, feats), BF16), sized((tok...  92.7 us
  transfers between devices with their start and end apart: 1, of which 0 were waited for; matrix products, arithmetic and copies ran while one was open for 2% of the time, Pallas kernels for 96%

profile of v1, /device:TPU:32, one launch (start us, length us, event | category | flops | bytes accessed | tf_op | source)
XLA Modules:
  0.0 255.5 jit_solution(15877996507639321740)
XLA Ops:
  0.6 3.1 %collective-permute-start = (s32[1,128]{1,0:T(1,128)}, s32[1,128]{1,0:T(1,128)S(1)}, u32[]{:S(2)}, u32[]{:S(2)}) collective-permute-start(s32[1,128]{1,0:T(1,128)} %param.16), channel_id=1, source_target_pairs={{0,128},{128,0},{1,129},{129,1},{2,130},{130,2},{3,131},{131,3},{4... | collective-permute-start | bytes 1544 | tf_op jit(solution)/shard_map/ppermute | solution.py:604
  3.7 0.7 convert_bitcast_fusion
  4.4 0.7 reduce-precision_convert_fusion.1
  5.1 0.7 fusion.1
  5.8 1.4 maximum_maximum_fusion.kvm
  7.2 0.7 broadcast_in_dim.19.segq
  7.9 92.7 %front.1 = (bf16[128,1024]{1,0:T(8,128)(2,1)}, bf16[128,1024]{1,0:T(8,128)(2,1)}, f32[16,512]{1,0:T(8,128)}, f32[16,512]{1,0:T(8,128)}, bf16[2,768,1024]{2,1,0:T(8,128)(2,1)}, /*index=5*/bf16[2,768,1024]{2,1,0:T(8,128)(2,1)}) custom-call(bf16[128,1024]{1,0:T(8,128)(2,1)} %bitcast.30, bf16[160,256]{1,0:T(8,128)(2,1)} %maximum_maximum_fusion.kvm, ...), custom_call_target="tpu_custom_call" | custom-call | tf_op jit(solution)/shard_map/front/pallas_call | solution.py:508
  100.6 152.7 %back.1 = bf16[128,1024]{1,0:T(8,128)(2,1)} custom-call(bf16[128,1024]{1,0:T(8,128)(2,1)} %get-tuple-element.8.xn, bf16[128,1024]{1,0:T(8,128)(2,1)} %get-tuple-element.9.resid, f32[16,512]{1,0:T(8,128)} %get-tuple-element.10.rank, f32[16,512]{1,0:T(8,128)} %get-tuple-element.11.share, bf16[2,768,1024]{2,1,0:T(8,128)(2,1)} %get-tuple-element.12.wg, ...), custom_call_target="tpu_custom_call" | custom-call | tf_op jit(solution)/shard_map/back/pallas_call | solution.py:548
  253.3 0.0 collective-permute-done
  253.3 1.7 copy.16
  255.0 0.5 copy.17
  (1 shorter events, 0.0 us)
Async XLA Ops:
  0.6 252.7 %collective-permute-start = (s32[1,128]{1,0:T(1,128)}, s32[1,128]{1,0:T(1,128)S(1)}, u32[]{:S(2)}, u32[]{:S(2)}) collective-permute-start(s32[1,128]{1,0:T(1,128)} %param.16), channel_id=1, source_target_pairs={{0,128},{128,0},{1,129},{129,1},{2,130},{130,2},{3,131},{131,3},{4... | collective-permute-start | bytes 1544 | tf_op jit(solution)/shard_map/ppermute | solution.py:604

commit v2 on v1

v2 whole, which is shorter than its diff:
```python
import math

import jax
import jax.numpy as jnp
from jax import lax
from jax.experimental import pallas as pl
from jax.experimental.pallas import tpu as pltpu
from jax.sharding import PartitionSpec as P

MESH = pl.DeviceIdType.MESH
HEAD = 128
NZ = 8
FOLD = 4
NEG = -1e30
EPS = 1e-06
CAP = 20
F32 = jnp.float32
BF16 = jnp.bfloat16


def place(x, z, c):
    return x * (2 * NZ) + lax.rem(z + 2 * NZ, NZ) * 2 + c


class Net:
    def __init__(self, send, recv):
        self.send_sems, self.recv_sems = send, recv
        cp = lax.axis_index("cp")
        self.cp = cp
        self.x = cp // (2 * NZ)
        self.z = (cp // 2) % NZ
        self.c = cp % 2
        self.f = lax.axis_index("fold")
        self.xp = 1 - self.x
        self.fp, self.fo, self.fm = [lax.rem(self.f + k, FOLD) for k in (1, 2, 3)]
        self.ids = {}
        self.sent = []

    def to(self, way):
        x, z, c = self.x, self.z, self.c
        if way == "z+":
            return {"cp": place(x, z + 1, c)}
        if way == "z-":
            return {"cp": place(x, z - 1, c)}
        if way == "x":
            return {"cp": place(1 - x, z, c)}
        if way == "c":
            return {"cp": place(x, z, 1 - c)}
        if way == "f+":
            return {"fold": self.fp}
        if way == "f-":
            return {"fold": self.fm}
        if way == "fo":
            return {"fold": self.fo}
        return {"section": 1 - lax.axis_index("section")}

    def greet(self, ways):
        for way in ways:
            pl.semaphore_signal(
                pltpu.get_barrier_semaphore(), inc=1, device_id=self.to(way), device_id_type=MESH
            )

    def meet(self, ways):
        pl.semaphore_wait(pltpu.get_barrier_semaphore(), len(ways))

    def slot(self, name):
        return self.ids.setdefault(name, len(self.ids))

    def copy(self, name, src, dst, way):
        i = self.slot(name)
        return pltpu.make_async_remote_copy(
            src_ref=src,
            dst_ref=dst,
            send_sem=self.send_sems.at[i],
            recv_sem=self.recv_sems.at[i],
            device_id=self.to(way),
            device_id_type=MESH,
        )

    def push(self, name, src, dst, way):
        copy = self.copy(name, src, dst, way)
        copy.start()
        self.sent.append((name[0], copy))

    def await_(self, name, dst, way):
        self.copy(name, dst, dst, way).wait_recv()

    def drain(self, *kinds):
        for kind, copy in self.sent:
            if not kinds or kind in kinds:
                copy.wait_send()
        self.sent = [entry for entry in self.sent if kinds and entry[0] not in kinds]


class Gather:
    def __init__(self, net, name, buf, rows1):
        self.net, self.name, self.buf = net, name, buf
        self.rows = buf.shape[1]
        self.rows1 = rows1

    def block(self, x, z, c, part="full"):
        ref = self.buf.at[place(x, z, c)]
        if part == "full":
            return ref
        if part == "r1":
            return ref.at[pl.ds(0, self.rows1)]
        return ref.at[pl.ds(self.rows1, self.rows - self.rows1)]

    def push(self, tag, key, way, part="full"):
        ref = self.block(*key, part)
        self.net.push((self.name, tag), ref, ref, way)

    def wait(self, tag, key, way, part="full"):
        self.net.await_((self.name, tag), self.block(*key, part), way)

    def tick(self, s):
        n = self.net
        x, z, c, xp, cp = n.x, n.z, n.c, n.xp, 1 - n.c
        if s == 0:
            for tag, way in (("zp0", "z+"), ("zm0", "z-"), ("x0", "x"), ("c0", "c")):
                self.push(tag, (x, z, c), way)
            return
        if s == 1:
            self.wait("x0", (xp, z, c), "x")
            self.push("yp0", (xp, z, c), "z+", "r2")
            self.push("ym0", (xp, z, c), "z-", "r2")
            self.push("cx0", (xp, z, c), "c")
        if s <= 4:
            self.wait(f"zp{s - 1}", (x, z - s, c), "z+")
            if s <= 3:
                self.push(f"zp{s}", (x, z - s, c), "z+")
                self.wait(f"zm{s - 1}", (x, z + s, c), "z-")
                if s <= 2:
                    self.push(f"zm{s}", (x, z + s, c), "z-")
            self.push(f"xm{s}", (x, z - s, c), "x", "r1")
            if s <= 3:
                self.push(f"xp{s}", (x, z + s, c), "x", "r1")
            self.push(f"cm{s}", (x, z - s, c), "c")
            if s <= 3:
                self.push(f"cp{s}", (x, z + s, c), "c")
        if s >= 2 and s <= 5:
            d = s - 1
            self.wait(f"ym{d - 1}", (xp, z + d, c), "z-", "r2")
            if d <= 3:
                self.push(f"ym{d}", (xp, z + d, c), "z-", "r2")
                self.wait(f"yp{d - 1}", (xp, z - d, c), "z+", "r2")
                if d <= 2:
                    self.push(f"yp{d}", (xp, z - d, c), "z+", "r2")
            self.push(f"dp{d}", (xp, z + d, c), "c", "r2")
            if d <= 3:
                self.push(f"dm{d}", (xp, z - d, c), "c", "r2")
            self.wait(f"xm{d}", (xp, z - d, c), "x", "r1")
            self.push(f"em{d}", (xp, z - d, c), "c", "r1")
            if d <= 3:
                self.wait(f"xp{d}", (xp, z + d, c), "x", "r1")
                self.push(f"ep{d}", (xp, z + d, c), "c", "r1")

    def ready(self, d):
        n = self.net
        x, z, xp, cp = n.x, n.z, n.xp, 1 - n.c
        if d == 0:
            self.wait("c0", (x, z, cp), "c")
            self.wait("cx0", (xp, z, cp), "c")
            return
        side, s = ("p", d) if d > 0 else ("m", -d)
        self.wait(f"c{side}{s}", (x, z + d, cp), "c")
        self.wait(f"d{'p' if s == 4 else side}{s}", (xp, z + d, cp), "c", "r2")
        self.wait(f"e{side}{s}", (xp, z + d, cp), "c", "r1")


DISTANCES = (0, -1, 1, -2, 2, -3, 3, -4)
STAGES = ((3, -4), (2, -3), (1, -2), (-1, 0))
WAYS = ("z+", "z-", "x", "c", "f+", "f-", "fo", "sec")
NT = (((1,), (1,)), ((), ()))


def layer(
    q, keys, values, segments, routes, weights, act, gain, wo, wg, wu, wd,
    passed, passed_segments,
    kvg, pool, xg, wgv, wuv, wdv, bias, attended, hits, rank, share, proj, pa, pb, pc, pd, stat,
    slots, part, ra, rb, rc, rd, hidden, result, cin, xin, zin, yin, tin, resid, done,
    send, recv, local,
):
    net = Net(send, recv)
    x, z, c, xp, cpeer = net.x, net.z, net.c, net.xp, 1 - net.c
    f, fp, fo, fm = net.f, net.fp, net.fo, net.fm
    tokens, feats = act.shape
    cap = 4 * CAP
    rows1 = tokens * 5 // 8
    rows2 = tokens - rows1
    net.greet(WAYS)

    kvg[net.cp, 0:tokens, 0:HEAD] = keys[...]
    kvg[net.cp, 0:tokens, HEAD:2 * HEAD] = values[...]
    weight = weights[...]
    first = weight.astype(BF16).astype(F32)
    second = (weight - first).astype(BF16).astype(F32)
    third = weight - first - second
    meta = jnp.concatenate([routes[...].astype(F32), first, second, third], axis=0)
    kvg[net.cp, tokens:tokens + 32, 0:HEAD] = meta.astype(BF16)
    side = jnp.broadcast_to(segments[...].astype(F32), (32, tokens)).astype(BF16)
    kvg[net.cp, tokens:tokens + 32, HEAD:2 * HEAD] = side
    eye = (
        lax.broadcasted_iota(jnp.int32, (tokens, tokens), 0) == lax.broadcasted_iota(jnp.int32, (tokens, tokens), 1)
    ).astype(F32).astype(BF16)
    seg_q = lax.dot_general(eye, side, NT, preferred_element_type=F32)[:, 0:1]
    pool[net.cp] = lax.dot_general(eye, wo[...], NT, preferred_element_type=F32).astype(BF16)

    net.meet(WAYS)
    kv = Gather(net, "kv", kvg, kvg.shape[1] * 3 // 5)
    out = Gather(net, "wo", pool, rows1)
    kv.tick(0)
    out.tick(0)
    hid = wg.shape[1]
    loads = [pltpu.make_async_copy(wd, wdv, local.at[2])]
    for k, (src, dst) in enumerate(((wg, wgv), (wu, wuv))):
        rows = pl.ds(f * hid, hid)
        for way, t in (("f+", fp), ("f-", fm), ("fo", fo)):
            net.push(("w", k, way), src.at[:, :, pl.ds(t * feats, feats)], dst.at[:, rows, :], way)
        loads.append(
            pltpu.make_async_copy(src.at[:, :, pl.ds(f * feats, feats)], dst.at[:, rows, :], local.at[k])
        )
    for copy in loads:
        copy.start()
    net.push(("seg",), segments, passed_segments, "sec")

    for s in range(1, 6):
        kv.tick(s)
        if s == 4:
            out.tick(1)
    for d in DISTANCES:
        kv.ready(d)
    out.tick(2)

    window = 17
    start = jnp.maximum(net.cp - (window - 1), 0)
    span = window * tokens
    seg_k = jnp.concatenate(
        [kvg[start + i, tokens:tokens + 16, HEAD:2 * HEAD].astype(F32)[0:1] for i in range(window)], axis=1
    )
    q_place = net.cp * tokens + lax.broadcasted_iota(jnp.int32, (tokens, span), 0)
    k_place = start * tokens + lax.broadcasted_iota(jnp.int32, (tokens, span), 1)
    allowed = (k_place <= q_place) & (seg_k == seg_q)
    bias[...] = jnp.where(allowed, 0.0, NEG)
    factor = math.log2(math.e) / math.sqrt(HEAD)

    def head(h, carry):
        columns = pl.ds(pl.multiple_of(h * HEAD, HEAD), HEAD)
        ks = kvg[pl.ds(start, window), 0:tokens, 0:HEAD].reshape(span, HEAD)
        vs = kvg[pl.ds(start, window), 0:tokens, HEAD:2 * HEAD].reshape(span, HEAD)
        score = lax.dot_general(q[:, columns], ks, NT, preferred_element_type=F32)
        score = score * factor + bias[...]
        top = jnp.max(score, axis=1, keepdims=True)
        terms = jnp.exp2(score - top)
        total = jnp.sum(terms, axis=1, keepdims=True)
        mixed = jnp.dot(terms.astype(BF16), vs, preferred_element_type=F32)
        attended[:, columns] = (mixed / total).astype(BF16)
        return carry

    heads = q.shape[1] // HEAD
    lax.fori_loop(0, heads // 2, head, 0)
    out.tick(3)
    lax.fori_loop(heads // 2, heads, head, 0)
    out.tick(4)
    out.tick(5)
    for d in DISTANCES:
        out.ready(d)

    per = 4 * NZ // FOLD

    def project(t):
        lhs = attended[...]
        for i in range(0, per, 2):
            rhs = pool[pl.ds(t * per + i, 2)].reshape(2 * tokens, lhs.shape[1])
            proj[t, :, i * tokens:(i + 2) * tokens] = lax.dot_general(
                lhs, rhs, NT, preferred_element_type=F32
            ).astype(BF16)

    half = feats // 2
    project(fo)
    net.push(("pa",), proj.at[fo, :, pl.ds(0, half)], pa, "f+")
    net.push(("pb",), proj.at[fo, :, pl.ds(half, half)], pb, "f-")
    project(fp)
    project(fm)
    net.await_(("pa",), pa, "f+")
    proj[fp, :, 0:half] = (proj[fp, :, 0:half].astype(F32) + pa[...].astype(F32)).astype(BF16)
    net.push(("pc",), proj.at[fp], pc, "f+")
    net.await_(("pb",), pb, "f-")
    proj[fm, :, half:2 * half] = (proj[fm, :, half:2 * half].astype(F32) + pb[...].astype(F32)).astype(BF16)
    net.push(("pd",), proj.at[fm], pd, "f-")
    project(f)
    base = act[...].astype(F32) + proj[f].astype(F32)
    net.await_(("pc",), pc, "f+")
    net.await_(("pd",), pd, "f-")
    kept = (base + pc[...].astype(F32) + pd[...].astype(F32)).astype(BF16)
    resid[...] = kept
    wide = kept.astype(F32)
    stat[0] = jnp.broadcast_to(jnp.sum(wide * wide, axis=1, keepdims=True), stat.shape[1:])
    for k, way in enumerate(("f+", "f-", "fo")):
        net.push(("s", k), stat.at[0], stat.at[k + 1], way)
    for k, way in enumerate(("f+", "f-", "fo")):
        net.await_(("s", k), stat.at[k + 1], way)
    total = (stat[0] + stat[1] + stat[2] + stat[3])[:, 0:1]
    scale = lax.rsqrt(total / (feats * FOLD) + EPS)
    xg[net.cp] = (wide * scale * gain[...].astype(F32)).astype(BF16)

    xs = Gather(net, "x", xg, rows1)
    xs.tick(0)

    for g in range(NZ):
        for e in range(2):
            expert = (2 * net.cp + e).astype(F32)
            for k in range(4):
                meta = kvg[place(k // 2, g, k % 2), tokens:tokens + 32, 0:tokens].astype(F32)
                chosen = meta[0:8] == expert
                row = pl.ds(2 * g + e, 1)
                columns = pl.ds(k * tokens, tokens)
                hits[row, columns] = jnp.sum(jnp.where(chosen, 1.0, 0.0), axis=0, keepdims=True)
                shares = meta[8:16] + meta[16:24] + meta[24:32]
                share[row, columns] = jnp.sum(jnp.where(chosen, shares, 0.0), axis=0, keepdims=True)
    xs.tick(1)
    wide4 = 4 * tokens
    earlier = lax.broadcasted_iota(jnp.int32, (wide4, wide4), 0) < lax.broadcasted_iota(jnp.int32, (wide4, wide4), 1)
    hit = hits[...]
    before = jnp.dot(hit.astype(BF16), jnp.where(earlier, 1.0, 0.0).astype(BF16), preferred_element_type=F32)
    rank[...] = jnp.where(hit > 0.5, before, -1.0)

    def group(d):
        return lax.rem(z + d + NZ, NZ)

    def pick(d, e):
        row = rank[pl.ds(2 * group(d) + e, 1), :]
        want = lax.broadcasted_iota(jnp.int32, (cap, 4 * tokens), 0).astype(F32)
        return jnp.where(want == row, 1.0, 0.0)

    def select(i):
        for j, d in enumerate(STAGES[i]):
            xs.ready(d)
            g = group(d)
            low = xg[pl.ds(2 * g, 2)].reshape(2 * tokens, feats)
            high = xg[pl.ds(2 * NZ + 2 * g, 2)].reshape(2 * tokens, feats)
            choice = jnp.concatenate([pick(d, 0), pick(d, 1)], axis=0).astype(BF16)
            got = jnp.dot(choice[:, 0:2 * tokens], low, preferred_element_type=F32)
            got = (got + jnp.dot(choice[:, 2 * tokens:], high, preferred_element_type=F32)).astype(BF16)
            for e in range(2):
                slots[i, pl.ds((2 * e + j) * cap, cap), :] = got[e * cap:(e + 1) * cap]

    wide_hid = FOLD * hid

    def enter(i):
        for e in range(2):
            lhs = slots[i, pl.ds(2 * e * cap, 2 * cap), :]
            for k, w in enumerate((wgv, wuv)):
                res = lax.dot_general(lhs, w[e], NT, preferred_element_type=F32).astype(BF16)
                part[i, 2 * e, :, k * wide_hid:(k + 1) * wide_hid] = res[0:cap]
                part[i, 2 * e + 1, :, k * wide_hid:(k + 1) * wide_hid] = res[cap:]
        net.push(("a", i), part.at[i, fo, :, pl.ds(0, wide_hid)], ra.at[i], "f+")
        net.push(("b", i), part.at[i, fo, :, pl.ds(wide_hid, wide_hid)], rb.at[i], "f-")

    def relay(i):
        left, right = pl.ds(0, wide_hid), pl.ds(wide_hid, wide_hid)
        net.await_(("a", i), ra.at[i], "f+")
        part[i, fp, :, left] = (part[i, fp, :, left].astype(F32) + ra[i].astype(F32)).astype(BF16)
        net.push(("c", i), part.at[i, fp], rc.at[i], "f+")
        net.await_(("b", i), rb.at[i], "f-")
        part[i, fm, :, right] = (part[i, fm, :, right].astype(F32) + rb[i].astype(F32)).astype(BF16)
        net.push(("d", i), part.at[i, fm], rd.at[i], "f-")

    def activate(i):
        net.await_(("c", i), rc.at[i], "f+")
        net.await_(("d", i), rd.at[i], "f-")
        total = part[i, f].astype(F32) + rc[i].astype(F32) + rd[i].astype(F32)
        gate, up = total[:, 0:wide_hid], total[:, wide_hid:2 * wide_hid]
        hidden[i, f] = (gate / (1.0 + jnp.exp(-gate)) * up).astype(BF16)
        net.push(("h+", i), hidden.at[i, f], hidden.at[i, f], "f+")
        net.push(("h-", i), hidden.at[i, f], hidden.at[i, f], "f-")

    half_hid = wide_hid // 2

    def spread(i):
        net.await_(("h+", i), hidden.at[i, fm], "f+")
        lower = hidden.at[i, fm, :, pl.ds(0, half_hid)]
        net.push(("i+", i), lower, lower, "f+")
        net.await_(("h-", i), hidden.at[i, fp], "f-")
        upper = hidden.at[i, fp, :, pl.ds(half_hid, half_hid)]
        net.push(("i-", i), upper, upper, "f-")

    def leave(i):
        net.await_(("i+", i), hidden.at[i, fo, :, pl.ds(0, half_hid)], "f+")
        net.await_(("i-", i), hidden.at[i, fo, :, pl.ds(half_hid, half_hid)], "f-")
        for e in range(2):
            lhs = hidden[i, 2 * e:2 * e + 2].reshape(2 * cap, wide_hid)
            res = jnp.dot(lhs, wdv[e], preferred_element_type=F32)
            for j, d in enumerate(STAGES[i]):
                row = share[pl.ds(2 * group(d) + e, 1), :]
                scaled = jnp.sum(pick(d, e) * row, axis=1, keepdims=True)
                result[2 * j + e] = (res[j * cap:(j + 1) * cap] * scaled).astype(BF16)
        for j, d in enumerate(STAGES[i]):
            g = group(d)
            choice = jnp.concatenate([pick(d, 0), pick(d, 1)], axis=0).astype(BF16)
            res = result[2 * j:2 * j + 2].reshape(2 * cap, feats)
            total = lax.dot_general(choice, res, (((0,), (0,)), ((), ())), preferred_element_type=F32).astype(BF16)
            for k in range(4):
                pool[place(k // 2, g, k % 2)] = total[k * tokens:(k + 1) * tokens]
            for xx in range(2):
                net.push(("rc", d, xx), pool.at[place(xx, g, cpeer)], cin.at[g, xx], "c")

    def accumulate(at, rows, inc):
        pool[at, rows] = (pool[at, rows].astype(F32) + inc.astype(F32)).astype(BF16)

    full, ahead, rest = pl.ds(0, tokens), pl.ds(0, rows1), pl.ds(rows1, rows2)

    def merge(i):
        for d in STAGES[i]:
            g = group(d)
            for xx in range(2):
                net.await_(("rc", d, xx), cin.at[g, xx], "c")
                accumulate(place(xx, g, c), full, cin[g, xx])
            net.push(("rx", d), pool.at[place(xp, g, c), ahead], xin.at[g], "x")

    def cross(d):
        g = group(d)
        net.await_(("rx", d), xin.at[g], "x")
        accumulate(place(x, g, c), ahead, xin[g])

    lines = (
        ("z-", -1, 4, x, zin, 0, full),
        ("z+", 1, 3, x, zin, 4, full),
        ("z-", -1, 3, xp, yin, 0, rest),
        ("z+", 1, 4, xp, yin, 3, rest),
    )

    def hop(k, d):
        way, sign, hops, line, inbox, first, rows = lines[k]
        s = hops - abs(d)
        at = place(line, z + d, c)
        if s > 0:
            net.await_(("rz", k, s - 1), inbox.at[first + s - 1], way)
            accumulate(at, rows, inbox[first + s - 1])
        if s < hops:
            net.push(("rz", k, s), pool.at[at, rows], inbox.at[first + s], way)

    xs.tick(2)
    xs.tick(3)
    select(3)
    xs.tick(4)
    select(2)
    xs.tick(5)
    select(1)
    select(0)
    net.drain("wo")
    for k, dst in enumerate((wgv, wuv)):
        for way, t in (("f+", fm), ("f-", fp), ("fo", fo)):
            net.await_(("w", k, way), dst.at[:, pl.ds(t * hid, hid), :], way)
    for copy in loads:
        copy.wait()

    enter(0)
    enter(1)
    relay(0)
    relay(1)
    activate(0)
    enter(2)
    activate(1)
    spread(0)
    relay(2)
    leave(0)
    spread(1)
    enter(3)
    activate(2)
    merge(0)
    leave(1)
    relay(3)
    spread(2)
    cross(-4)
    hop(0, -4)
    hop(3, 4)
    cross(3)
    hop(1, 3)
    merge(1)
    activate(3)
    leave(2)
    cross(-3)
    hop(0, -3)
    hop(2, -3)
    hop(3, 3)
    cross(2)
    spread(3)
    hop(1, 2)
    merge(2)
    hop(3, 2)
    leave(3)
    cross(1)
    hop(1, 1)
    hop(3, 1)
    cross(-2)
    hop(0, -2)
    hop(2, -2)
    merge(3)
    cross(-1)
    hop(0, -1)
    hop(2, -1)
    cross(0)
    hop(3, 0)
    hop(1, 0)
    hop(2, 0)
    net.push(("rt",), pool.at[place(xp, z, c), rest], tin, "x")
    hop(0, 0)
    own = resid[...].astype(F32) + pool[net.cp].astype(F32)
    net.await_(("rt",), tin, "x")
    done[0:rows1] = own[0:rows1].astype(BF16)
    done[rows1:tokens] = (own[rows1:] + tin[...].astype(F32)).astype(BF16)
    net.push(("out",), done, passed, "sec")
    net.await_(("seg",), passed_segments, "sec")
    net.await_(("out",), passed, "sec")
    net.drain()


def run_layer(q, keys, values, segments, routes, weights, act, gain, wo, wg, wu, wd):
    tokens, feats = act.shape
    blocks = 4 * NZ
    experts, quarter, wide = wg.shape
    hid = quarter * FOLD
    cap = 4 * CAP
    rows1 = tokens * 5 // 8
    dma = pltpu.SemaphoreType.DMA

    def scratch(*shape, dtype=BF16):
        return pltpu.VMEM(shape, dtype)

    vmem, hbm = pl.BlockSpec(memory_space=pltpu.VMEM), pl.BlockSpec(memory_space=pl.ANY)
    return pl.pallas_call(
        layer,
        out_shape=(jax.ShapeDtypeStruct((tokens, feats), BF16), jax.ShapeDtypeStruct(segments.shape, segments.dtype)),
        in_specs=[vmem] * 9 + [hbm] * 3,
        out_specs=(vmem, vmem),
        scratch_shapes=[
            scratch(blocks, tokens + 32, 2 * HEAD),
            scratch(blocks, tokens, feats),
            scratch(blocks, tokens, feats),
            scratch(experts, hid, feats),
            scratch(experts, hid, feats),
            scratch(experts, hid, feats),
            scratch(tokens, 17 * tokens, dtype=F32),
            scratch(*q.shape),
            scratch(2 * NZ, 4 * tokens, dtype=F32),
            scratch(2 * NZ, 4 * tokens, dtype=F32),
            scratch(2 * NZ, 4 * tokens, dtype=F32),
            scratch(FOLD, tokens, feats),
            scratch(tokens, feats // 2),
            scratch(tokens, feats // 2),
            scratch(tokens, feats),
            scratch(tokens, feats),
            scratch(4, tokens, 128, dtype=F32),
            scratch(4, 4 * cap, feats),
            scratch(4, FOLD, cap, 2 * hid),
            scratch(4, cap, hid),
            scratch(4, cap, hid),
            scratch(4, cap, 2 * hid),
            scratch(4, cap, 2 * hid),
            scratch(4, FOLD, cap, hid),
            scratch(4, cap, feats),
            scratch(NZ, 2, tokens, feats),
            scratch(NZ, rows1, feats),
            scratch(7, tokens, feats),
            scratch(7, tokens - rows1, feats),
            scratch(tokens - rows1, feats),
            scratch(tokens, feats),
            scratch(tokens, feats),
            dma((224,)),
            dma((224,)),
            dma((3,)),
        ],
        compiler_params=pltpu.CompilerParams(collective_id=0, has_side_effects=True, vmem_limit_bytes=62 * 2**20),
        name="layer",
    )(q, keys, values, segments, routes, weights, act, gain, wo, wg, wu, wd)


def body(
    activations, queries, keys, values, segments, routes, route_weight, norm_gain, w_out, w_gate, w_up, w_down,
):
    passed, moved = run_layer(
        queries[0], keys[0], values[0], segments, routes[0].T, route_weight[0].T, activations[0], norm_gain,
        w_out[0], w_gate[0], w_up[0], w_down[0],
    )
    return passed[None], moved


def solution(mesh):
    return jax.shard_map(
        body,
        mesh=mesh,
        in_specs=(
            P("section", "cp", "fold"),
            P("section", "cp", "fold"),
            P("section", "cp", "fold"),
            P("section", "cp", "fold"),
            P("section", "cp"),
            P("section", "cp", None),
            P("section", "cp", None),
            P("section", "fold"),
            P("section", "fold", "cp"),
            P("section", "cp", "fold", None),
            P("section", "cp", "fold", None),
            P("section", "cp", None, "fold"),
        ),
        out_specs=(P("section", "cp", "fold"), P("section", "cp")),
        check_vma=False,
    )
```

time: 257 us -> 227 us (0.88)
  Pallas kernels: 245 us -> 223 us
  other arithmetic: 3.49 us -> 0 us
  starting transfers between devices: 3.11 us -> 0 us
    pallas_call x2 -> x1, Pallas kernels: 245 us -> 223 us  [run_layer(): pl.pallas_call(layer, out_shape=(jax.ShapeDtypeStruct((tokens, feats), BF...]
    ppermute x1 -> x0, starting transfers between devices: 3.11 us -> none  [body(): moved = lax.ppermute(segments, 'section', [(0, 1), (1, 0)])]
  transfers between devices with their start and end apart: 1 -> 0, of which waited for: 0 -> 0; matrix products, arithmetic and copies ran while one was open for 2% -> 0% of each run, Pallas kernels for 96% -> 0%
where the time goes in v2:
time: 227 us
  Pallas kernels  223 us (98%)
  local copies, waits for them, and re-layouts  2.8 us (1%)
    pallas_call x1, Pallas kernels, run_layer(): pl.pallas_call(layer, out_shape=(jax.ShapeDtypeStruct((tokens, feats), BF...  223 us

profile of v2, /device:TPU:32, one launch (start us, length us, event | category | flops | bytes accessed | tf_op | source)
XLA Modules:
  0.0 226.9 jit_solution(2167684645244024805)
XLA Ops:
  0.6 223.5 %layer.1 = (bf16[128,1024]{1,0:T(8,128)(2,1)}, s32[1,128]{1,0:T(1,128)}) custom-call(bf16[128,1024]{1,0:T(8,128)(2,1)} %bitcast.18, bf16[128,128]{1,0:T(8,128)(2,1)} %bitcast.22, bf16[128,128]{1,0:T(8,128)(2,1)} %bitcast.23, s32[1,128]{1,0:T(1,128)} %segments.1, s32[8,128]{1,0:T(8,128)} %bitcast.24, f32[8,128]{1,0:T(8,128)} %bitcast.25, ...), custom_call_target="tpu_custom_call" | custom-call | tf_op jit(solution)/shard_map/layer/pallas_call | solution.py:532
  224.1 1.7 copy.16
  225.8 1.1 copy.17

commit v3 on v2

--- a/solution.py
+++ b/solution.py
@@ -177,7 +177,7 @@
 def layer(
     q, keys, values, segments, routes, weights, act, gain, wo, wg, wu, wd,
     passed, passed_segments,
-    kvg, pool, xg, wgv, wuv, wdv, bias, attended, hits, rank, share, proj, pa, pb, pc, pd, stat,
+    kvg, pool, xg, wgv, wuv, wdv, qs, top, total, mixed, attended, hits, rank, share, proj, inbox, stat,
     slots, part, ra, rb, rc, rd, hidden, result, cin, xin, zin, yin, tin, resid, done,
     send, recv, local,
 ):
@@ -193,21 +193,20 @@
     kvg[net.cp, 0:tokens, 0:HEAD] = keys[...]
     kvg[net.cp, 0:tokens, HEAD:2 * HEAD] = values[...]
     weight = weights[...]
-    first = weight.astype(BF16).astype(F32)
-    second = (weight - first).astype(BF16).astype(F32)
-    third = weight - first - second
-    meta = jnp.concatenate([routes[...].astype(F32), first, second, third], axis=0)
-    kvg[net.cp, tokens:tokens + 32, 0:HEAD] = meta.astype(BF16)
-    side = jnp.broadcast_to(segments[...].astype(F32), (32, tokens)).astype(BF16)
-    kvg[net.cp, tokens:tokens + 32, HEAD:2 * HEAD] = side
+    coarse = weight.astype(BF16).astype(F32)
+    side = jnp.broadcast_to(segments[...].astype(F32), (8, tokens))
+    meta = jnp.concatenate([routes[...].astype(F32), coarse], axis=0)
+    kvg[net.cp, tokens:tokens + 16, 0:HEAD] = meta.astype(BF16)
+    meta = jnp.concatenate([weight - coarse, side], axis=0)
+    kvg[net.cp, tokens:tokens + 16, HEAD:2 * HEAD] = meta.astype(BF16)
     eye = (
         lax.broadcasted_iota(jnp.int32, (tokens, tokens), 0) == lax.broadcasted_iota(jnp.int32, (tokens, tokens), 1)
     ).astype(F32).astype(BF16)
-    seg_q = lax.dot_general(eye, side, NT, preferred_element_type=F32)[:, 0:1]
+    seg_q = lax.dot_general(eye, jnp.concatenate([side, side], axis=0).astype(BF16), NT, preferred_element_type=F32)[:, 0:1]
     pool[net.cp] = lax.dot_general(eye, wo[...], NT, preferred_element_type=F32).astype(BF16)
 
     net.meet(WAYS)
-    kv = Gather(net, "kv", kvg, kvg.shape[1] * 3 // 5)
+    kv = Gather(net, "kv", kvg, rows1)
     out = Gather(net, "wo", pool, rows1)
     kv.tick(0)
     out.tick(0)
@@ -215,53 +214,75 @@
     loads = [pltpu.make_async_copy(wd, wdv, local.at[2])]
     for k, (src, dst) in enumerate(((wg, wgv), (wu, wuv))):
         rows = pl.ds(f * hid, hid)
-        for way, t in (("f+", fp), ("f-", fm), ("fo", fo)):
-            net.push(("w", k, way), src.at[:, :, pl.ds(t * feats, feats)], dst.at[:, rows, :], way)
         loads.append(
             pltpu.make_async_copy(src.at[:, :, pl.ds(f * feats, feats)], dst.at[:, rows, :], local.at[k])
         )
     for copy in loads:
         copy.start()
+
+    def resplit(k, src, dst):
+        for way, t in (("f+", fp), ("f-", fm), ("fo", fo)):
+            net.push(("w", k, way), src.at[:, :, pl.ds(t * feats, feats)], dst.at[:, pl.ds(f * hid, hid), :], way)
+
+    resplit(0, wg, wgv)
     net.push(("seg",), segments, passed_segments, "sec")
 
-    for s in range(1, 6):
-        kv.tick(s)
-        if s == 4:
-            out.tick(1)
-    for d in DISTANCES:
-        kv.ready(d)
+    heads = q.shape[1] // HEAD
+    for h in range(heads):
+        qs[h] = q[:, h * HEAD:(h + 1) * HEAD]
+    top[...] = jnp.full(top.shape, NEG, F32)
+    total[...] = jnp.zeros(total.shape, F32)
+    mixed[...] = jnp.zeros(mixed.shape, F32)
+    factor = math.log2(math.e) / math.sqrt(HEAD)
+    q_place = net.cp * tokens + lax.broadcasted_iota(jnp.int32, (tokens, 2 * tokens), 0)
+
+    def attend(line, d):
+        base = place(line, z + d, 0)
+        ks = kvg[pl.ds(base, 2), 0:tokens, 0:HEAD].reshape(2 * tokens, HEAD)
+        vs = kvg[pl.ds(base, 2), 0:tokens, HEAD:2 * HEAD].reshape(2 * tokens, HEAD)
+        seg_k = jnp.concatenate(
+            [kvg[base + i, tokens:tokens + 16, HEAD:2 * HEAD].astype(F32)[8:9] for i in range(2)], axis=1
+        )
+        k_place = base * tokens + lax.broadcasted_iota(jnp.int32, (tokens, 2 * tokens), 1)
+        bias = jnp.where((k_place <= q_place) & (seg_k == seg_q), 0.0, NEG)
+        score = lax.dot_general(qs[...].reshape(heads * tokens, HEAD), ks, NT, preferred_element_type=F32)
+        score = score.reshape(heads, tokens, 2 * tokens) * factor + bias[None]
+        old = top[...]
+        new = jnp.maximum(old, jnp.max(score, axis=2, keepdims=True))
+        terms = jnp.exp2(score - new[:, :, 0:1])
+        fade = jnp.exp2(old - new)
+        top[...] = new
+        total[...] = total[...] * fade + jnp.sum(terms, axis=2, keepdims=True)
+        more = jnp.dot(
+            terms.astype(BF16).reshape(heads * tokens, 2 * tokens), vs, preferred_element_type=F32
+        ).reshape(heads, tokens, HEAD)
+        mixed[...] = mixed[...] * fade + more
+
+    def attend_to(*distances):
+        for d in distances:
+            kv.ready(d)
+            if d == 0:
+                attend(x, 0)
+                attend(xp, 0)
+            else:
+                attend(jnp.where(lax.rem(z + d + NZ, NZ) < z, x, 0), d)
+
+    kv.tick(1)
+    kv.tick(2)
+    out.tick(1)
+    attend_to(0)
+    kv.tick(3)
+    attend_to(-1, 1)
     out.tick(2)
-
-    window = 17
-    start = jnp.maximum(net.cp - (window - 1), 0)
-    span = window * tokens
-    seg_k = jnp.concatenate(
-        [kvg[start + i, tokens:tokens + 16, HEAD:2 * HEAD].astype(F32)[0:1] for i in range(window)], axis=1
-    )
-    q_place = net.cp * tokens + lax.broadcasted_iota(jnp.int32, (tokens, span), 0)
-    k_place = start * tokens + lax.broadcasted_iota(jnp.int32, (tokens, span), 1)
-    allowed = (k_place <= q_place) & (seg_k == seg_q)
-    bias[...] = jnp.where(allowed, 0.0, NEG)
-    factor = math.log2(math.e) / math.sqrt(HEAD)
-
-    def head(h, carry):
-        columns = pl.ds(pl.multiple_of(h * HEAD, HEAD), HEAD)
-        ks = kvg[pl.ds(start, window), 0:tokens, 0:HEAD].reshape(span, HEAD)
-        vs = kvg[pl.ds(start, window), 0:tokens, HEAD:2 * HEAD].reshape(span, HEAD)
-        score = lax.dot_general(q[:, columns], ks, NT, preferred_element_type=F32)
-        score = score * factor + bias[...]
-        top = jnp.max(score, axis=1, keepdims=True)
-        terms = jnp.exp2(score - top)
-        total = jnp.sum(terms, axis=1, keepdims=True)
-        mixed = jnp.dot(terms.astype(BF16), vs, preferred_element_type=F32)
-        attended[:, columns] = (mixed / total).astype(BF16)
-        return carry
-
-    heads = q.shape[1] // HEAD
-    lax.fori_loop(0, heads // 2, head, 0)
+    kv.tick(4)
+    attend_to(-2, 2)
     out.tick(3)
-    lax.fori_loop(heads // 2, heads, head, 0)
+    kv.tick(5)
+    attend_to(-3, 3)
     out.tick(4)
+    attend_to(-4)
+    for h in range(heads):
+        attended[:, h * HEAD:(h + 1) * HEAD] = (mixed[h] / total[h]).astype(BF16)
     out.tick(5)
     for d in DISTANCES:
         out.ready(d)
@@ -276,47 +297,48 @@
                 lhs, rhs, NT, preferred_element_type=F32
             ).astype(BF16)
 
-    half = feats // 2
+    ways = (("f+", fp, fm), ("f-", fm, fp), ("fo", fo, fo))
     project(fo)
-    net.push(("pa",), proj.at[fo, :, pl.ds(0, half)], pa, "f+")
-    net.push(("pb",), proj.at[fo, :, pl.ds(half, half)], pb, "f-")
+    net.push(("p", 2), proj.at[fo], inbox.at[2], "fo")
     project(fp)
+    net.push(("p", 0), proj.at[fp], inbox.at[0], "f+")
     project(fm)
-    net.await_(("pa",), pa, "f+")
-    proj[fp, :, 0:half] = (proj[fp, :, 0:half].astype(F32) + pa[...].astype(F32)).astype(BF16)
-    net.push(("pc",), proj.at[fp], pc, "f+")
-    net.await_(("pb",), pb, "f-")
-    proj[fm, :, half:2 * half] = (proj[fm, :, half:2 * half].astype(F32) + pb[...].astype(F32)).astype(BF16)
-    net.push(("pd",), proj.at[fm], pd, "f-")
+    net.push(("p", 1), proj.at[fm], inbox.at[1], "f-")
     project(f)
     base = act[...].astype(F32) + proj[f].astype(F32)
-    net.await_(("pc",), pc, "f+")
-    net.await_(("pd",), pd, "f-")
-    kept = (base + pc[...].astype(F32) + pd[...].astype(F32)).astype(BF16)
+    for k, way in enumerate(("f+", "f-", "fo")):
+        net.await_(("p", k), inbox.at[k], way)
+        base = base + inbox[k].astype(F32)
+    kept = base.astype(BF16)
     resid[...] = kept
     wide = kept.astype(F32)
-    stat[0] = jnp.broadcast_to(jnp.sum(wide * wide, axis=1, keepdims=True), stat.shape[1:])
+    stat[0] = lax.dot_general(
+        jnp.ones((8, feats), F32), wide * wide, NT, preferred_element_type=F32, precision=lax.Precision.HIGHEST
+    )
     for k, way in enumerate(("f+", "f-", "fo")):
         net.push(("s", k), stat.at[0], stat.at[k + 1], way)
+    normed = wide * gain[...].astype(F32)
     for k, way in enumerate(("f+", "f-", "fo")):
         net.await_(("s", k), stat.at[k + 1], way)
-    total = (stat[0] + stat[1] + stat[2] + stat[3])[:, 0:1]
-    scale = lax.rsqrt(total / (feats * FOLD) + EPS)
-    xg[net.cp] = (wide * scale * gain[...].astype(F32)).astype(BF16)
+    squares = stat[0] + stat[1] + stat[2] + stat[3]
+    scale = lax.rsqrt(squares / (feats * FOLD) + EPS)
+    scale = lax.dot_general(eye.astype(F32), scale, NT, preferred_element_type=F32, precision=lax.Precision.HIGHEST)
+    xg[net.cp] = (normed * scale[:, 0:1]).astype(BF16)
 
     xs = Gather(net, "x", xg, rows1)
     xs.tick(0)
+    resplit(1, wu, wuv)
 
     for g in range(NZ):
         for e in range(2):
             expert = (2 * net.cp + e).astype(F32)
             for k in range(4):
-                meta = kvg[place(k // 2, g, k % 2), tokens:tokens + 32, 0:tokens].astype(F32)
-                chosen = meta[0:8] == expert
+                meta = kvg[place(k // 2, g, k % 2), tokens:tokens + 16].astype(F32)
+                chosen = meta[0:8, 0:tokens] == expert
                 row = pl.ds(2 * g + e, 1)
                 columns = pl.ds(k * tokens, tokens)
                 hits[row, columns] = jnp.sum(jnp.where(chosen, 1.0, 0.0), axis=0, keepdims=True)
-                shares = meta[8:16] + meta[16:24] + meta[24:32]
+                shares = meta[8:16, 0:tokens] + meta[0:8, tokens:2 * tokens]
                 share[row, columns] = jnp.sum(jnp.where(chosen, shares, 0.0), axis=0, keepdims=True)
     xs.tick(1)
     wide4 = 4 * tokens
@@ -369,8 +391,8 @@
     def activate(i):
         net.await_(("c", i), rc.at[i], "f+")
         net.await_(("d", i), rd.at[i], "f-")
-        total = part[i, f].astype(F32) + rc[i].astype(F32) + rd[i].astype(F32)
-        gate, up = total[:, 0:wide_hid], total[:, wide_hid:2 * wide_hid]
+        both = part[i, f].astype(F32) + rc[i].astype(F32) + rd[i].astype(F32)
+        gate, up = both[:, 0:wide_hid], both[:, wide_hid:2 * wide_hid]
         hidden[i, f] = (gate / (1.0 + jnp.exp(-gate)) * up).astype(BF16)
         net.push(("h+", i), hidden.at[i, f], hidden.at[i, f], "f+")
         net.push(("h-", i), hidden.at[i, f], hidden.at[i, f], "f-")
@@ -399,9 +421,9 @@
             g = group(d)
             choice = jnp.concatenate([pick(d, 0), pick(d, 1)], axis=0).astype(BF16)
             res = result[2 * j:2 * j + 2].reshape(2 * cap, feats)
-            total = lax.dot_general(choice, res, (((0,), (0,)), ((), ())), preferred_element_type=F32).astype(BF16)
+            summed = lax.dot_general(choice, res, (((0,), (0,)), ((), ())), preferred_element_type=F32).astype(BF16)
             for k in range(4):
-                pool[place(k // 2, g, k % 2)] = total[k * tokens:(k + 1) * tokens]
+                pool[place(k // 2, g, k % 2)] = summed[k * tokens:(k + 1) * tokens]
             for xx in range(2):
                 net.push(("rc", d, xx), pool.at[place(xx, g, cpeer)], cin.at[g, xx], "c")
 
@@ -507,12 +529,14 @@
     net.push(("rt",), pool.at[place(xp, z, c), rest], tin, "x")
     hop(0, 0)
     own = resid[...].astype(F32) + pool[net.cp].astype(F32)
+    done[ahead] = own[0:rows1].astype(BF16)
+    net.push(("out", 0), done.at[ahead], passed.at[ahead], "sec")
     net.await_(("rt",), tin, "x")
-    done[0:rows1] = own[0:rows1].astype(BF16)
-    done[rows1:tokens] = (own[rows1:] + tin[...].astype(F32)).astype(BF16)
-    net.push(("out",), done, passed, "sec")
+    done[rest] = (own[rows1:] + tin[...].astype(F32)).astype(BF16)
+    net.push(("out", 1), done.at[rest], passed.at[rest], "sec")
     net.await_(("seg",), passed_segments, "sec")
-    net.await_(("out",), passed, "sec")
+    net.await_(("out", 0), passed.at[ahead], "sec")
+    net.await_(("out", 1), passed.at[rest], "sec")
     net.drain()
 
 
@@ -522,6 +546,7 @@
     experts, quarter, wide = wg.shape
     hid = quarter * FOLD
     cap = 4 * CAP
+    heads = q.shape[1] // HEAD
     rows1 = tokens * 5 // 8
     dma = pltpu.SemaphoreType.DMA
 
@@ -535,23 +560,23 @@
         in_specs=[vmem] * 9 + [hbm] * 3,
         out_specs=(vmem, vmem),
         scratch_shapes=[
-            scratch(blocks, tokens + 32, 2 * HEAD),
+            scratch(blocks, tokens + 16, 2 * HEAD),
             scratch(blocks, tokens, feats),
             scratch(blocks, tokens, feats),
             scratch(experts, hid, feats),
             scratch(experts, hid, feats),
             scratch(experts, hid, feats),
-            scratch(tokens, 17 * tokens, dtype=F32),
+            scratch(heads, tokens, HEAD),
+            scratch(heads, tokens, HEAD, dtype=F32),
+            scratch(heads, tokens, HEAD, dtype=F32),
+            scratch(heads, tokens, HEAD, dtype=F32),
             scratch(*q.shape),
             scratch(2 * NZ, 4 * tokens, dtype=F32),
             scratch(2 * NZ, 4 * tokens, dtype=F32),
             scratch(2 * NZ, 4 * tokens, dtype=F32),
             scratch(FOLD, tokens, feats),
-            scratch(tokens, feats // 2),
-            scratch(tokens, feats // 2),
-            scratch(tokens, feats),
-            scratch(tokens, feats),
-            scratch(4, tokens, 128, dtype=F32),
+            scratch(3, tokens, feats),
+            scratch(4, 8, tokens, dtype=F32),
             scratch(4, 4 * cap, feats),
             scratch(4, FOLD, cap, 2 * hid),
             scratch(4, cap, hid),

time: 227 us -> 204 us (0.90)
  Pallas kernels: 223 us -> 200 us
    pallas_call x1, Pallas kernels: 223 us -> 200 us  [run_layer(): pl.pallas_call(layer, out_shape=(jax.ShapeDtypeStruct((tokens, feats), BF...]
where the time goes in v3:
time: 204 us; the launch traced here: 203 us
  Pallas kernels  200 us (98%)
  local copies, waits for them, and re-layouts  2.8 us (1%)
    pallas_call x1, Pallas kernels, run_layer(): pl.pallas_call(layer, out_shape=(jax.ShapeDtypeStruct((tokens, feats), BF...  200 us

profile of v3, /device:TPU:32, one launch (start us, length us, event | category | flops | bytes accessed | tf_op | source)
XLA Modules:
  0.0 203.0 jit_solution(11389399683629153415)
XLA Ops:
  0.6 199.6 %layer.1 = (bf16[128,1024]{1,0:T(8,128)(2,1)}, s32[1,128]{1,0:T(1,128)}) custom-call(bf16[128,1024]{1,0:T(8,128)(2,1)} %bitcast.18, bf16[128,128]{1,0:T(8,128)(2,1)} %bitcast.22, bf16[128,128]{1,0:T(8,128)(2,1)} %bitcast.23, s32[1,128]{1,0:T(1,128)} %segments.1, s32[8,128]{1,0:T(8,128)} %bitcast.24, f32[8,128]{1,0:T(8,128)} %bitcast.25, ...), custom_call_target="tpu_custom_call" | custom-call | tf_op jit(solution)/shard_map/layer/pallas_call | solution.py:557
  200.2 1.7 copy.16
  201.9 1.1 copy.17

commit v4 on v3

--- a/solution.py
+++ b/solution.py
@@ -126,18 +126,21 @@
             self.push("ym0", (xp, z, c), "z-", "r2")
             self.push("cx0", (xp, z, c), "c")
         if s <= 4:
-            self.wait(f"zp{s - 1}", (x, z - s, c), "z+")
+            near = "full" if s <= 3 else "r1"
+            self.wait(f"zp{s - 1}", (x, z - s, c), "z+", near)
             if s <= 3:
-                self.push(f"zp{s}", (x, z - s, c), "z+")
+                self.push(f"zp{s}", (x, z - s, c), "z+", "full" if s <= 2 else "r1")
                 self.wait(f"zm{s - 1}", (x, z + s, c), "z-")
-                if s <= 2:
-                    self.push(f"zm{s}", (x, z + s, c), "z-")
+                self.push(f"zm{s}", (x, z + s, c), "z-", "full" if s <= 2 else "r2")
             self.push(f"xm{s}", (x, z - s, c), "x", "r1")
             if s <= 3:
                 self.push(f"xp{s}", (x, z + s, c), "x", "r1")
-            self.push(f"cm{s}", (x, z - s, c), "c")
+            self.push(f"cm{s}", (x, z - s, c), "c", near)
             if s <= 3:
                 self.push(f"cp{s}", (x, z + s, c), "c")
+            else:
+                self.wait("zm3", (x, z + 4, c), "z-", "r2")
+                self.push("cn4", (x, z + 4, c), "c", "r2")
         if s >= 2 and s <= 5:
             d = s - 1
             self.wait(f"ym{d - 1}", (xp, z + d, c), "z-", "r2")
@@ -163,7 +166,9 @@
             self.wait("cx0", (xp, z, cp), "c")
             return
         side, s = ("p", d) if d > 0 else ("m", -d)
-        self.wait(f"c{side}{s}", (x, z + d, cp), "c")
+        self.wait(f"c{side}{s}", (x, z + d, cp), "c", "full" if s <= 3 else "r1")
+        if s == 4:
+            self.wait("cn4", (x, z + d, cp), "c", "r2")
         self.wait(f"d{'p' if s == 4 else side}{s}", (xp, z + d, cp), "c", "r2")
         self.wait(f"e{side}{s}", (xp, z + d, cp), "c", "r1")
 
@@ -177,9 +182,9 @@
 def layer(
     q, keys, values, segments, routes, weights, act, gain, wo, wg, wu, wd,
     passed, passed_segments,
-    kvg, pool, xg, wgv, wuv, wdv, qs, top, total, mixed, attended, hits, rank, share, proj, inbox, stat,
+    kvg, pool, xg, wgv, wuv, wdv, qs, top, total, mixed, attended, hits, rank, share, proj, mine, inbox, stat,
     slots, part, ra, rb, rc, rd, hidden, result, cin, xin, zin, yin, tin, resid, done,
-    send, recv, local,
+    send, recv, pair_send, pair_recv, local,
 ):
     net = Net(send, recv)
     x, z, c, xp, cpeer = net.x, net.z, net.c, net.xp, 1 - net.c
@@ -269,45 +274,75 @@
 
     kv.tick(1)
     kv.tick(2)
-    out.tick(1)
     attend_to(0)
     kv.tick(3)
+    out.tick(1)
     attend_to(-1, 1)
+    kv.tick(4)
     out.tick(2)
-    kv.tick(4)
     attend_to(-2, 2)
-    out.tick(3)
     kv.tick(5)
     attend_to(-3, 3)
-    out.tick(4)
+    out.tick(3)
     attend_to(-4)
     for h in range(heads):
         attended[:, h * HEAD:(h + 1) * HEAD] = (mixed[h] / total[h]).astype(BF16)
+
+    pairs = [(line, d) for d in DISTANCES for line in range(2)]
+    per = 4 * NZ // FOLD
+    two = 2 * tokens
+
+    def owner(line, d):
+        base = place(line, z + d, 0)
+        t = base // per
+        return base, lax.rem(t - f + FOLD, FOLD), base % per
+
+    def shipment(n, line, d):
+        base, k, column = owner(line, d)
+        return pltpu.make_async_remote_copy(
+            src_ref=proj.at[n],
+            dst_ref=inbox.at[k - 1, :, pl.ds(pl.multiple_of(column * tokens, two), two)],
+            send_sem=pair_send.at[n],
+            recv_sem=pair_recv.at[(k - 1) * 4 + column // 2],
+            device_id={"fold": base // per},
+            device_id_type=MESH,
+        )
+
+    def project_to(*distances):
+        for d in distances:
+            out.ready(d)
+            for line in range(2):
+                n = pairs.index((line, d))
+                base, k, column = owner(line, d)
+                rhs = pool[pl.ds(base, 2)].reshape(two, attended.shape[1])
+                res = lax.dot_general(attended[...], rhs, NT, preferred_element_type=F32).astype(BF16)
+                proj[n] = res
+
+                @pl.when(k == 0)
+                def _():
+                    mine[:, pl.ds(pl.multiple_of(column * tokens, two), two)] = res
+
+                @pl.when(k != 0)
+                def _():
+                    shipment(n, line, d).start()
+
+    project_to(0, -1, 1)
+    out.tick(4)
+    project_to(-2, 2)
     out.tick(5)
-    for d in DISTANCES:
-        out.ready(d)
-
-    per = 4 * NZ // FOLD
-
-    def project(t):
-        lhs = attended[...]
-        for i in range(0, per, 2):
-            rhs = pool[pl.ds(t * per + i, 2)].reshape(2 * tokens, lhs.shape[1])
-            proj[t, :, i * tokens:(i + 2) * tokens] = lax.dot_general(
-                lhs, rhs, NT, preferred_element_type=F32
-            ).astype(BF16)
-
-    ways = (("f+", fp, fm), ("f-", fm, fp), ("fo", fo, fo))
-    project(fo)
-    net.push(("p", 2), proj.at[fo], inbox.at[2], "fo")
-    project(fp)
-    net.push(("p", 0), proj.at[fp], inbox.at[0], "f+")
-    project(fm)
-    net.push(("p", 1), proj.at[fm], inbox.at[1], "f-")
-    project(f)
-    base = act[...].astype(F32) + proj[f].astype(F32)
-    for k, way in enumerate(("f+", "f-", "fo")):
-        net.await_(("p", k), inbox.at[k], way)
+    project_to(-3, 3, -4)
+    base = act[...].astype(F32) + mine[...].astype(F32)
+    for k in range(3):
+        for j in range(4):
+            block = inbox.at[k, :, pl.ds(j * two, two)]
+            pltpu.make_async_remote_copy(
+                src_ref=block,
+                dst_ref=block,
+                send_sem=pair_send.at[0],
+                recv_sem=pair_recv.at[k * 4 + j],
+                device_id={"fold": fp},
+                device_id_type=MESH,
+            ).wait_recv()
         base = base + inbox[k].astype(F32)
     kept = base.astype(BF16)
     resid[...] = kept
@@ -369,15 +404,24 @@
 
     wide_hid = FOLD * hid
 
-    def enter(i):
+    def enter(i, k):
+        w = (wgv, wuv)[k]
+        columns = pl.ds(k * wide_hid, wide_hid)
         for e in range(2):
             lhs = slots[i, pl.ds(2 * e * cap, 2 * cap), :]
-            for k, w in enumerate((wgv, wuv)):
-                res = lax.dot_general(lhs, w[e], NT, preferred_element_type=F32).astype(BF16)
-                part[i, 2 * e, :, k * wide_hid:(k + 1) * wide_hid] = res[0:cap]
-                part[i, 2 * e + 1, :, k * wide_hid:(k + 1) * wide_hid] = res[cap:]
-        net.push(("a", i), part.at[i, fo, :, pl.ds(0, wide_hid)], ra.at[i], "f+")
-        net.push(("b", i), part.at[i, fo, :, pl.ds(wide_hid, wide_hid)], rb.at[i], "f-")
+            res = lax.dot_general(lhs, w[e], NT, preferred_element_type=F32).astype(BF16)
+            part[i, 2 * e, :, columns] = res[0:cap]
+            part[i, 2 * e + 1, :, columns] = res[cap:]
+        if k == 0:
+            net.push(("a", i), part.at[i, fo, :, columns], ra.at[i], "f+")
+        else:
+            net.push(("b", i), part.at[i, fo, :, columns], rb.at[i], "f-")
+
+    def have(k):
+        dst = (wgv, wuv)[k]
+        for way, t in (("f+", fm), ("f-", fp), ("fo", fo)):
+            net.await_(("w", k, way), dst.at[:, pl.ds(t * hid, hid), :], way)
+        loads[k + 1].wait()
 
     def relay(i):
         left, right = pl.ds(0, wide_hid), pl.ds(wide_hid, wide_hid)
@@ -410,30 +454,35 @@
     def leave(i):
         net.await_(("i+", i), hidden.at[i, fo, :, pl.ds(0, half_hid)], "f+")
         net.await_(("i-", i), hidden.at[i, fo, :, pl.ds(half_hid, half_hid)], "f-")
-        for e in range(2):
-            lhs = hidden[i, 2 * e:2 * e + 2].reshape(2 * cap, wide_hid)
-            res = jnp.dot(lhs, wdv[e], preferred_element_type=F32)
-            for j, d in enumerate(STAGES[i]):
-                row = share[pl.ds(2 * group(d) + e, 1), :]
-                scaled = jnp.sum(pick(d, e) * row, axis=1, keepdims=True)
-                result[2 * j + e] = (res[j * cap:(j + 1) * cap] * scaled).astype(BF16)
-        for j, d in enumerate(STAGES[i]):
-            g = group(d)
-            choice = jnp.concatenate([pick(d, 0), pick(d, 1)], axis=0).astype(BF16)
-            res = result[2 * j:2 * j + 2].reshape(2 * cap, feats)
-            summed = lax.dot_general(choice, res, (((0,), (0,)), ((), ())), preferred_element_type=F32).astype(BF16)
-            for k in range(4):
-                pool[place(k // 2, g, k % 2)] = summed[k * tokens:(k + 1) * tokens]
-            for xx in range(2):
-                net.push(("rc", d, xx), pool.at[place(xx, g, cpeer)], cin.at[g, xx], "c")
+        for group_ids in ((0, 1),) if i < 3 else ((0,), (1,)):
+            for e in range(2):
+                lhs = hidden[i, pl.ds(2 * e + group_ids[0], len(group_ids))].reshape(len(group_ids) * cap, wide_hid)
+                res = jnp.dot(lhs, wdv[e], preferred_element_type=F32)
+                for n, j in enumerate(group_ids):
+                    d = STAGES[i][j]
+                    row = share[pl.ds(2 * group(d) + e, 1), :]
+                    scaled = jnp.sum(pick(d, e) * row, axis=1, keepdims=True)
+                    result[2 * j + e] = (res[n * cap:(n + 1) * cap] * scaled).astype(BF16)
+            for j in group_ids:
+                d = STAGES[i][j]
+                g = group(d)
+                choice = jnp.concatenate([pick(d, 0), pick(d, 1)], axis=0).astype(BF16)
+                res = result[2 * j:2 * j + 2].reshape(2 * cap, feats)
+                summed = lax.dot_general(
+                    choice, res, (((0,), (0,)), ((), ())), preferred_element_type=F32
+                ).astype(BF16)
+                for k in range(4):
+                    pool[place(k // 2, g, k % 2)] = summed[k * tokens:(k + 1) * tokens]
+                for xx in range(2):
+                    net.push(("rc", d, xx), pool.at[place(xx, g, cpeer)], cin.at[g, xx], "c")
 
     def accumulate(at, rows, inc):
         pool[at, rows] = (pool[at, rows].astype(F32) + inc.astype(F32)).astype(BF16)
 
     full, ahead, rest = pl.ds(0, tokens), pl.ds(0, rows1), pl.ds(rows1, rows2)
 
-    def merge(i):
-        for d in STAGES[i]:
+    def merge(*distances):
+        for d in distances:
             g = group(d)
             for xx in range(2):
                 net.await_(("rc", d, xx), cin.at[g, xx], "c")
@@ -446,10 +495,12 @@
         accumulate(place(x, g, c), ahead, xin[g])
 
     lines = (
-        ("z-", -1, 4, x, zin, 0, full),
-        ("z+", 1, 3, x, zin, 4, full),
-        ("z-", -1, 3, xp, yin, 0, rest),
-        ("z+", 1, 4, xp, yin, 3, rest),
+        ("z-", -1, 4, x, zin, 0, ahead),
+        ("z+", 1, 3, x, zin, 4, ahead),
+        ("z-", -1, 3, x, yin, 0, rest),
+        ("z+", 1, 4, x, yin, 3, rest),
+        ("z-", -1, 3, xp, yin, 7, rest),
+        ("z+", 1, 4, xp, yin, 10, rest),
     )
 
     def hop(k, d):
@@ -467,66 +518,77 @@
     select(3)
     xs.tick(4)
     select(2)
+    have(0)
     xs.tick(5)
     select(1)
     select(0)
     net.drain("wo")
-    for k, dst in enumerate((wgv, wuv)):
-        for way, t in (("f+", fm), ("f-", fp), ("fo", fo)):
-            net.await_(("w", k, way), dst.at[:, pl.ds(t * hid, hid), :], way)
-    for copy in loads:
-        copy.wait()
-
-    enter(0)
-    enter(1)
+    enter(0, 0)
+    enter(1, 0)
+    have(1)
+    loads[0].wait()
+    enter(0, 1)
+    enter(1, 1)
     relay(0)
     relay(1)
     activate(0)
-    enter(2)
+    enter(2, 0)
+    enter(2, 1)
     activate(1)
     spread(0)
     relay(2)
     leave(0)
     spread(1)
-    enter(3)
+    enter(3, 0)
+    enter(3, 1)
     activate(2)
-    merge(0)
+    merge(-4, 3)
+    hop(3, 4)
+    hop(5, 4)
     leave(1)
     relay(3)
     spread(2)
     cross(-4)
     hop(0, -4)
-    hop(3, 4)
     cross(3)
     hop(1, 3)
-    merge(1)
+    merge(-3, 2)
+    hop(2, -3)
+    hop(4, -3)
     activate(3)
     leave(2)
+    hop(3, 3)
+    hop(5, 3)
     cross(-3)
     hop(0, -3)
-    hop(2, -3)
-    hop(3, 3)
     cross(2)
     spread(3)
     hop(1, 2)
-    merge(2)
+    merge(-2, 1)
+    hop(2, -2)
+    hop(4, -2)
     hop(3, 2)
+    hop(5, 2)
     leave(3)
     cross(1)
+    cross(-2)
+    hop(0, -2)
     hop(1, 1)
     hop(3, 1)
-    cross(-2)
-    hop(0, -2)
-    hop(2, -2)
-    merge(3)
+    hop(5, 1)
+    merge(-1)
+    hop(2, -1)
+    hop(4, -1)
     cross(-1)
     hop(0, -1)
-    hop(2, -1)
+    merge(0)
+    hop(5, 0)
+    hop(4, 0)
+    net.push(("rt",), pool.at[place(xp, z, c), rest], tin, "x")
+    hop(3, 0)
+    hop(2, 0)
     cross(0)
-    hop(3, 0)
     hop(1, 0)
-    hop(2, 0)
-    net.push(("rt",), pool.at[place(xp, z, c), rest], tin, "x")
     hop(0, 0)
     own = resid[...].astype(F32) + pool[net.cp].astype(F32)
     done[ahead] = own[0:rows1].astype(BF16)
@@ -538,6 +600,10 @@
     net.await_(("out", 0), passed.at[ahead], "sec")
     net.await_(("out", 1), passed.at[rest], "sec")
     net.drain()
+    for n, (line, d) in enumerate(pairs):
+        @pl.when(owner(line, d)[1] != 0)
+        def _():
+            shipment(n, line, d).wait_send()
 
 
 def run_layer(q, keys, values, segments, routes, weights, act, gain, wo, wg, wu, wd):
@@ -574,7 +640,8 @@
             scratch(2 * NZ, 4 * tokens, dtype=F32),
             scratch(2 * NZ, 4 * tokens, dtype=F32),
             scratch(2 * NZ, 4 * tokens, dtype=F32),
-            scratch(FOLD, tokens, feats),
+            scratch(2 * NZ, tokens, 2 * tokens),
+            scratch(tokens, feats),
             scratch(3, tokens, feats),
             scratch(4, 8, tokens, dtype=F32),
             scratch(4, 4 * cap, feats),
@@ -587,13 +654,15 @@
             scratch(4, cap, feats),
             scratch(NZ, 2, tokens, feats),
             scratch(NZ, rows1, feats),
-            scratch(7, tokens, feats),
-            scratch(7, tokens - rows1, feats),
+            scratch(7, rows1, feats),
+            scratch(14, tokens - rows1, feats),
             scratch(tokens - rows1, feats),
             scratch(tokens, feats),
             scratch(tokens, feats),
-            dma((224,)),
-            dma((224,)),
+            dma((240,)),
+            dma((240,)),
+            dma((2 * NZ,)),
+            dma((12,)),
             dma((3,)),
         ],
         compiler_params=pltpu.CompilerParams(collective_id=0, has_side_effects=True, vmem_limit_bytes=62 * 2**20),

time: 204 us -> 195 us (0.956)
  Pallas kernels: 200 us -> 190 us
    pallas_call x1, Pallas kernels: 200 us -> 190 us  [run_layer(): pl.pallas_call(layer, out_shape=(jax.ShapeDtypeStruct((tokens, feats), BF...]
where the time goes in v4:
time: 195 us; the launch traced here: 194 us
  Pallas kernels  190 us (97%)
  local copies, waits for them, and re-layouts  2.8 us (1%)
    pallas_call x1, Pallas kernels, run_layer(): pl.pallas_call(layer, out_shape=(jax.ShapeDtypeStruct((tokens, feats), BF...  190 us

profile of v4, /device:TPU:32, one launch (start us, length us, event | category | flops | bytes accessed | tf_op | source)
XLA Modules:
  0.0 193.9 jit_solution(2925757769669042763)
XLA Ops:
  0.6 190.5 %layer.1 = (bf16[128,1024]{1,0:T(8,128)(2,1)}, s32[1,128]{1,0:T(1,128)}) custom-call(bf16[128,1024]{1,0:T(8,128)(2,1)} %bitcast.18, bf16[128,128]{1,0:T(8,128)(2,1)} %bitcast.22, bf16[128,128]{1,0:T(8,128)(2,1)} %bitcast.23, s32[1,128]{1,0:T(1,128)} %segments.1, s32[8,128]{1,0:T(8,128)} %bitcast.24, f32[8,128]{1,0:T(8,128)} %bitcast.25, ...), custom_call_target="tpu_custom_call" | custom-call | tf_op jit(solution)/shard_map/layer/pallas_call | solution.py:623
  191.1 1.7 copy.16
  192.8 1.1 copy.17

commit v5 on v4

--- a/solution.py
+++ b/solution.py
@@ -412,10 +412,14 @@
             res = lax.dot_general(lhs, w[e], NT, preferred_element_type=F32).astype(BF16)
             part[i, 2 * e, :, columns] = res[0:cap]
             part[i, 2 * e + 1, :, columns] = res[cap:]
-        if k == 0:
-            net.push(("a", i), part.at[i, fo, :, columns], ra.at[i], "f+")
-        else:
-            net.push(("b", i), part.at[i, fo, :, columns], rb.at[i], "f-")
+
+    def gate(i):
+        enter(i, 0)
+
+    def up(i):
+        enter(i, 1)
+        net.push(("a", i), part.at[i, fo, :, pl.ds(0, wide_hid)], ra.at[i], "f+")
+        net.push(("b", i), part.at[i, fo, :, pl.ds(wide_hid, wide_hid)], rb.at[i], "f-")
 
     def have(k):
         dst = (wgv, wuv)[k]
@@ -514,33 +518,33 @@
             net.push(("rz", k, s), pool.at[at, rows], inbox.at[first + s], way)
 
     xs.tick(2)
+    have(0)
     xs.tick(3)
     select(3)
+    gate(3)
     xs.tick(4)
     select(2)
-    have(0)
+    gate(2)
     xs.tick(5)
     select(1)
+    gate(1)
     select(0)
     net.drain("wo")
-    enter(0, 0)
-    enter(1, 0)
+    gate(0)
     have(1)
     loads[0].wait()
-    enter(0, 1)
-    enter(1, 1)
+    up(0)
+    up(1)
     relay(0)
     relay(1)
     activate(0)
-    enter(2, 0)
-    enter(2, 1)
+    up(2)
     activate(1)
     spread(0)
     relay(2)
     leave(0)
     spread(1)
-    enter(3, 0)
-    enter(3, 1)
+    up(3)
     activate(2)
     merge(-4, 3)
     hop(3, 4)

time: 195 us -> 194 us (level)
  Pallas kernels: 190 us -> 188 us
    pallas_call x1, Pallas kernels: 190 us -> 188 us  [run_layer(): pl.pallas_call(layer, out_shape=(jax.ShapeDtypeStruct((tokens, feats), BF...]
where the time goes in v5:
time: 194 us; the launch traced here: 191 us
  Pallas kernels  188 us (97%)
  local copies, waits for them, and re-layouts  2.8 us (1%)
    pallas_call x1, Pallas kernels, run_layer(): pl.pallas_call(layer, out_shape=(jax.ShapeDtypeStruct((tokens, feats), BF...  188 us

profile of v5, /device:TPU:32, one launch (start us, length us, event | category | flops | bytes accessed | tf_op | source)
XLA Modules:
  0.0 191.2 jit_solution(5888816685722444009)
XLA Ops:
  0.6 187.8 %layer.1 = (bf16[128,1024]{1,0:T(8,128)(2,1)}, s32[1,128]{1,0:T(1,128)}) custom-call(bf16[128,1024]{1,0:T(8,128)(2,1)} %bitcast.18, bf16[128,128]{1,0:T(8,128)(2,1)} %bitcast.22, bf16[128,128]{1,0:T(8,128)(2,1)} %bitcast.23, s32[1,128]{1,0:T(1,128)} %segments.1, s32[8,128]{1,0:T(8,128)} %bitcast.24, f32[8,128]{1,0:T(8,128)} %bitcast.25, ...), custom_call_target="tpu_custom_call" | custom-call | tf_op jit(solution)/shard_map/layer/pallas_call | solution.py:627
  188.4 1.7 copy.16
  190.1 1.1 copy.17
